TPU v7x, 32 devices: a whole 2x2x4 slice. The times are simulated.
32 devices in a mesh: row: 8 (over z, core), col: 4 (over y, x).
Axes of the slice: x: 2, y: 2, z: 4, core: 2. Of those that a mesh axis runs over, the one named last changes fastest.
Arguments:
- spans: bfloat16 [4096, 768], P(('row', 'col')), may hold values from -10 to 10
- centroids: bfloat16 [2048, 768], P(('col', 'row')), may hold values from -10 to 10
- pattern: int32 [32, 4], P('row'), may hold values from 0 to 15, as said below
Outputs:
- new_centroids: bfloat16 [2048, 768], P(('col', 'row'))
- row_potential: float32 [4096], P('row')
- col_potential: float32 [2048], P('col')
Inputs may be any that keep to these rules, and one draw needn't show every extreme that they name: `pattern`: each row lists 4 distinct centroid blocks in rising order; row b always lists block b % 16; every centroid block is listed by some row.
All inputs are finite; a program needn't handle non-finite values.
Results may differ from a plain program's by a relative error of at most 0.0095.
Values may be sent and summed in bfloat16 or wider, within the bound.
No kernel may reach another device: no remote copies, remote signals or barrier semaphores. Data moves between devices by JAX's collectives and lax.ppermute only.
A program may use at most 64 MiB of HBM per device.

v0:
```python
import math

import jax
import jax.numpy as jnp
from jax import lax
from jax.sharding import PartitionSpec as P

ITERS = 3


logit_scale = 0.0625
floor_value = -1e30


def swap(x, axis, k):
    return lax.ppermute(x, axis, [(i, i ^ k) for i in range(lax.axis_size(axis))])


def swap_by_core(x, axis, for_core):
    cols = lax.axis_size("col")
    scale = cols if axis == "row" else 1
    pairs = [(i, i ^ (for_core[i // cols & 1] * scale)) for i in range(lax.axis_size("row") * cols)]
    return lax.ppermute(x, ("row", "col"), pairs)


def stages(axis):
    low = 1 if axis == "row" else 0
    bits = (lax.axis_size(axis) - 1).bit_length()
    return [(at, 1 << min(2, bits - at)) for at in range(low, bits, 2)]


def digit(axis, at, size):
    return (lax.axis_index(axis) >> at) & (size - 1)


def gather_spans(x, core):
    parts = [x]
    ready = x
    for at, size in stages("col"):
        x = jnp.concatenate(parts)
        parts = [x] + [swap(x, "col", d << at) for d in range(1, min(size, 3))]
        near = parts
        if size == 4:
            passed_on = jnp.where(core == 1, parts[2], parts[1])
            near = lax.optimization_barrier((parts, passed_on))[0]
            ready = passed_on
            parts = parts + [swap_by_core(passed_on, "col", (2 << at, 1 << at))]
    mate = [swap(part, "row", 1) for part in [jnp.concatenate(near)] + parts[3:]]
    return parts, mate, ready


def after(x, other):
    return lax.optimization_barrier((x, other))[0]


def placed(parts, index):
    whole = jnp.zeros((len(parts),) + parts[0].shape, parts[0].dtype)
    for d, part in enumerate(parts):
        whole = lax.dynamic_update_index_in_dim(whole, part, index ^ d, 0)
    return whole.reshape((-1,) + parts[0].shape[1:])


def gather_centroids(x, first, arrived):
    for at, size in stages("row"):
        sent = after(x, first)
        parts = [sent] + [swap(sent, "row", d << at) for d in range(1, size)]
        parts = [after(part, arrived) for part in parts]
        mate = [swap(part, "row", 1) for part in parts]
        position = digit("row", at, size)
        x = placed(parts, position)
    return jnp.concatenate([x, placed(mate, position)])


def reorder(x, blocks, k):
    x = x.reshape((blocks, -1) + x.shape[1:])
    return jnp.concatenate([x[p ^ k] for p in range(blocks)])


def unxor(x, index, blocks):
    shape = x.shape
    bit = 1
    while bit < blocks:
        pairs = x.reshape((blocks // (2 * bit), 2, -1) + shape[1:])
        x = jnp.where((index & bit) != 0, pairs[:, ::-1], pairs).reshape(shape)
        bit *= 2
    return x


def unxor_list(parts, index):
    bit = 1
    while bit < len(parts):
        parts = [jnp.where((index & bit) != 0, parts[p ^ bit], part) for p, part in enumerate(parts)]
        bit *= 2
    return parts


def tree(op, parts):
    while len(parts) > 1:
        parts = [op(parts[i], parts[i + 1]) for i in range(0, len(parts), 2)]
    return parts[0]


def add(parts):
    return tree(jnp.add, parts)


def log_sum(parts):
    high = tree(jnp.maximum, parts)
    return high + jnp.log(add([jnp.exp(part - high) for part in parts]))


def over_rows(merge, x):
    for at, size in stages("row"):
        x = merge([x] + [swap(x, "row", d << at) for d in range(1, size)])
    return x


def over_cols(merge, x):
    cols = lax.axis_size("col")
    for at, size in stages("col"):
        parts = [x]
        for d in range(1, size):
            halves = swap(x, "col", d << at).reshape(2, -1)
            parts.append(jnp.concatenate([reorder(half, cols, d << at) for half in halves]))
        x = merge(parts)
    return x


def in_thirds(x, width):
    thirds = []
    for step in range(3):
        top = lax.reduce_precision(x, 8, 7)
        thirds.append(top.astype(jnp.bfloat16))
        x = x - top
    return jnp.pad(jnp.stack(thirds), ((0, 5), (0, width - x.shape[0])))


def from_thirds(rows, count):
    thirds = rows[:3, :count].astype(jnp.float32)
    return thirds[0] + thirds[1] + thirds[2]


def per_device(spans, centroids, pattern):
    rows, cols = lax.axis_size("row"), lax.axis_size("col")
    chips = rows // 2
    me_row, me_col = lax.axis_index("row"), lax.axis_index("col")
    core = me_row % 2
    per, width = centroids.shape
    half_cols = per * chips
    group_cols = 2 * half_cols
    row_count = spans.shape[0] * cols
    mass_ratio = group_cols * cols / (row_count * rows)
    target = 1 / mass_ratio

    mate_pattern = swap(pattern, "row", 1)
    own_parts, mate_parts, ready = gather_spans(spans, core)
    tile_centroids = gather_centroids(centroids, mate_pattern, mate_parts[0])
    own_parts = [after(own_parts[0], mate_parts[0])] + own_parts[1:]
    span_halves = [jnp.concatenate(own_parts), jnp.concatenate(mate_parts)]
    at = jnp.arange(group_cols)
    row_of = at % half_cols // per * 2 + (at // half_cols ^ core)
    blocks = jnp.arange(group_cols // 128)
    in_block = ((row_of * per + at % per) // 128 == blocks[:, None]).astype(jnp.bfloat16)

    def half_scores(lists, span_half):
        listed = jnp.any(lists[:, :, None] == me_col * blocks.shape[0] + blocks, axis=1)
        listed = unxor(jnp.repeat(listed, 128 // spans.shape[0], axis=0).astype(jnp.bfloat16), me_col, cols)
        allowed_cells = jnp.dot(
            jnp.repeat(listed, spans.shape[0], axis=0), in_block, preferred_element_type=jnp.float32
        )
        products = lax.dot_general(
            span_half, tile_centroids, (((1,), (1,)), ((), ())), preferred_element_type=jnp.float32
        )
        return jnp.where(allowed_cells > 0.5, products * logit_scale, floor_value)

    scores = [half_scores(pattern, span_halves[0]), half_scores(mate_pattern, span_halves[1])]

    def with_rows(row_pot):
        return [half + row_pot[n * row_count : (n + 1) * row_count, None] for n, half in enumerate(scores)]

    def row_sums(row_pot, col_pot):
        return jnp.concatenate([jnp.sum(jnp.exp(x + col_pot[None, :]), axis=1) for x in with_rows(row_pot)])

    def col_sums(row_pot, col_pot):
        return add([jnp.sum(jnp.exp(x + col_pot[None, :]), axis=0) for x in with_rows(row_pot)])

    def rounds():
        highs = [jnp.max(half, axis=1) for half in scores]
        totals = [jnp.sum(jnp.exp(half - high[:, None]), axis=1) for half, high in zip(scores, highs)]
        row_pot = -over_cols(log_sum, jnp.concatenate([high + jnp.log(total) for high, total in zip(highs, totals)]))
        high = tree(jnp.maximum, [jnp.max(x, axis=0) for x in with_rows(row_pot)])
        total = col_sums(row_pot, -high)
        col_pot = math.log(target) - over_rows(log_sum, high + jnp.log(total))
        for sweep in range(1, ITERS):
            row_pot = row_pot - jnp.log(over_cols(add, row_sums(row_pot, col_pot)))
            if sweep < ITERS - 1:
                mass = over_rows(add, col_sums(row_pot, col_pot))
                col_pot = col_pot + math.log(target) - jnp.log(mass)
        return jnp.concatenate([row_pot.reshape(-1, group_cols), col_pot[None]])

    def nothing():
        return jnp.zeros((2 * row_count // group_cols + 1, group_cols), jnp.float32)

    known = lax.cond(core == 1, rounds, nothing)
    got = swap(known, "row", 1)
    row_pot = jnp.where(core == 1, known[:-1].reshape(-1), reorder(got[:-1].reshape(-1), 2, 1))
    col_pot = jnp.where(core == 1, known[-1], reorder(got[-1], 2, 1))

    mass = col_sums(row_pot, col_pot)
    held = add(
        [
            lax.dot_general(
                jnp.exp(x[:, :half_cols] + col_pot[None, :half_cols]).astype(jnp.bfloat16),
                span_half,
                (((0,), (0,)), ((), ())),
                preferred_element_type=jnp.float32,
            )
            for x, span_half in zip(with_rows(row_pot), span_halves)
        ]
    ).reshape(chips, per, width)
    for at, size in stages("row"):
        me = digit("row", at, size)
        held = held.reshape((-1, size) + held.shape[1:])
        low = held.astype(jnp.bfloat16)
        note = in_thirds(mass, width)
        parts, masses = [lax.dynamic_index_in_dim(held, me, 1, keepdims=False)], [from_thirds(note, group_cols)]
        for d in range(1, size):
            block = lax.dynamic_index_in_dim(low, me ^ d, 1, keepdims=False).reshape(-1, width)
            got = swap(jnp.concatenate([block, note]), "row", d << at)
            if d << at == 2:
                row_out = after(row_pot[:row_count], got)
                row_out = jnp.concatenate(unxor_list(jnp.split(row_out, cols), me_col))
            parts.append(got[: block.shape[0]].astype(jnp.float32).reshape(parts[0].shape))
            masses.append(from_thirds(got[block.shape[0] :], group_cols))
        held, mass = add(parts), add(masses)
    own_mass = lax.dynamic_slice_in_dim(mass, me_row // 2 * per, per, 0)
    col_pots = (col_pot + math.log(target) - jnp.log(mass)).reshape(2, chips, per)
    col_pots = jnp.where(core == 1, col_pots[::-1], col_pots)
    return (
        (held.reshape(per, width) * (target * mass_ratio / own_mass)[:, None]).astype(jnp.bfloat16),
        row_out,
        col_pots.swapaxes(0, 1).reshape(-1),
    )


def solution(mesh):
    placed = (P(("row", "col"), None), P(("col", "row"), None), P("row", None))
    return jax.shard_map(
        per_device,
        mesh=mesh,
        in_specs=placed,
        out_specs=(P(("col", "row"), None), P("row"), P("col")),
        check_vma=False,
    )
```

profile of v0, /device:TPU:0, one launch (start us, length us, event | category | flops | bytes accessed | tf_op | source)
XLA Modules:
  0.0 69.8 jit_solution(3130015822115301847)
XLA Ops:
  0.6 3.0 %collective-permute-start.16 = (bf16[128,768]{1,0:T(8,128)(2,1)}, bf16[128,768]{1,0:T(8,128)(2,1)S(1)}, u32[]{:S(2)}, u32[]{:S(2)}) collective-permute-start(bf16[128,768]{1,0:T(8,128)(2,1)} %param.5), channel_id=1, source_target_pairs={{0,2},{1,3},{2,0},{3,1},{4,6},{5,7},{6,4},{7,5},{8,10},{9,11},{10,... | collective-permute-start | bytes 589832 | tf_op jit(solution)/shard_map/ppermute | solution.py:16
  3.7 1.5 %collective-permute-start.15 = (bf16[128,768]{1,0:T(8,128)(2,1)}, bf16[128,768]{1,0:T(8,128)(2,1)S(1)}, u32[]{:S(2)}, u32[]{:S(2)}) collective-permute-start(bf16[128,768]{1,0:T(8,128)(2,1)} %param.5), channel_id=1, source_target_pairs={{0,1},{1,0},{2,3},{3,2},{4,5},{5,4},{6,7},{7,6},{8,9},{9,8},{10,11... | collective-permute-start | bytes 589832 | tf_op jit(solution)/shard_map/ppermute | solution.py:16
  5.2 1.3 %collective-permute-done.19 = s32[4,4]{1,0:T(4,128)S(1)} collective-permute-done((s32[4,4]{1,0:T(4,128)}, s32[4,4]{1,0:T(4,128)S(1)}, u32[]{:S(2)}, u32[]{:S(2)}) %collective-permute-start.19) | collective-permute-done | bytes 96 | tf_op jit(solution)/shard_map/ppermute | solution.py:16
  6.5 3.6 %collective-permute-start.22 = (bf16[64,768]{1,0:T(8,128)(2,1)}, bf16[64,768]{1,0:T(8,128)(2,1)S(1)}, u32[]{:S(2)}, u32[]{:S(2)}) collective-permute-start(bf16[64,768]{1,0:T(8,128)(2,1)} %param.6), channel_id=1, source_target_pairs={{0,24},{4,28},{8,16},{12,20},{16,8},{20,12},{24,0},{28,4},{1,25},{... | collective-permute-start | bytes 294920 | tf_op jit(solution)/shard_map/ppermute | solution.py:16
  10.1 0.8 %collective-permute-start.20 = (bf16[64,768]{1,0:T(8,128)(2,1)}, bf16[64,768]{1,0:T(8,128)(2,1)S(1)}, u32[]{:S(2)}, u32[]{:S(2)}) collective-permute-start(bf16[64,768]{1,0:T(8,128)(2,1)} %param.6), channel_id=1, source_target_pairs={{0,8},{4,12},{8,0},{12,4},{16,24},{20,28},{24,16},{28,20},{1,9},{5... | collective-permute-start | bytes 294920 | tf_op jit(solution)/shard_map/ppermute | solution.py:16
  10.9 0.8 %compare_reduce_fusion = (pred[4,4]{1,0:T(4,128)(4,1)S(1)}, pred[4,4]{1,0:T(4,128)(4,1)S(1)}) fusion(s32[4,4]{1,0:T(4,128)S(1)} %collective-permute-done.19, s32[4]{0:T(128)S(1)} %iota_add_fusion, s32[4,4]{1,0:T(4,128)} %param.7), kind=kLoop, calls=%fused_computation.139 | loop fusion | flops 224 | bytes 176 | tf_op jit(solution)/shard_map/reduce_or | solution.py:166
  11.8 1.0 %pad_maximum_fusion.6 = bf16[384,768]{1,0:T(8,128)(2,1)S(1)} fusion(bf16[128,768]{1,0:T(8,128)(2,1)S(1)} %collective-permute-done.16, bf16[128,768]{1,0:T(8,128)(2,1)S(1)} %collective-permute-done.15, bf16[128,768]{1,0:T(8,128)(2,1)} %param.5), kind=kLoop, calls=%fused_computation.99 | loop fusion | flops 1769472 | bytes 1179648 | tf_op jit(solution)/shard_map/concatenate | solution.py:48
  12.9 0.3 convolution_compare_fusion.1
  13.2 0.6 collective-permute-start.18
  13.8 0.3 convolution_compare_fusion
  14.1 4.8 %collective-permute-done.18 = bf16[128,768]{1,0:T(8,128)(2,1)S(1)} collective-permute-done((bf16[128,768]{1,0:T(8,128)(2,1)S(1)}, bf16[128,768]{1,0:T(8,128)(2,1)S(1)}, u32[]{:S(2)}, u32[]{:S(2)}) %collective-permute-start.18) | collective-permute-done | bytes 196640 | tf_op jit(solution)/shard_map/ppermute | solution.py:23
  19.0 0.6 collective-permute-start.23
  19.6 0.4 collective-permute-start.25
  20.6 0.3 collective-permute-done.24
  20.9 0.1 collective-permute-done.25
  21.0 0.3 collective-permute-done.26
  21.4 0.6 fusion.10
  22.0 0.6 fusion.11
  22.7 28.6 %collective-permute-start.28 = (f32[3,512]{1,0:T(4,128)S(1)}, f32[3,512]{1,0:T(4,128)S(1)}, u32[]{:S(2)}, u32[]{:S(2)}) collective-permute-start(f32[3,512]{1,0:T(4,128)S(1)} %get-tuple-element.102), channel_id=1, source_target_pairs={{0,4},{4,0},{8,12},{12,8},{16,20},{20,16},{24,28},{28,24},{1,5},{5... | collective-permute-start | bytes 18440 | tf_op jit(solution)/shard_map/ppermute | solution.py:16
  51.2 0.8 %collective-permute-done.28 = f32[3,512]{1,0:T(4,128)S(1)} collective-permute-done((f32[3,512]{1,0:T(4,128)S(1)}, f32[3,512]{1,0:T(4,128)S(1)}, u32[]{:S(2)}, u32[]{:S(2)}) %collective-permute-start.28) | collective-permute-done | bytes 6176 | tf_op jit(solution)/shard_map/ppermute | solution.py:16
  52.2 0.4 exponential_reduce_fusion.10
  52.6 0.7 copy-done.1
  53.3 0.4 fusion.16
  53.7 0.4 convolution_add_fusion
  54.3 1.8 %collective-permute-start.29 = (bf16[72,768]{1,0:T(8,128)(2,1)S(1)}, bf16[72,768]{1,0:T(8,128)(2,1)S(1)}, u32[]{:S(2)}, u32[]{:S(2)}) collective-permute-start(bf16[72,768]{1,0:T(8,128)(2,1)S(1)} %get-tuple-element.88), channel_id=1, source_target_pairs={{0,8},{4,12},{8,0},{12,4},{16,24},{20,28},{24,16},{28,20},{1,9},{5... | collective-permute-start | bytes 331784 | tf_op jit(solution)/shard_map/ppermute | solution.py:16
  56.3 1.2 %collective-permute-start.30 = (bf16[72,768]{1,0:T(8,128)(2,1)S(1)}, bf16[72,768]{1,0:T(8,128)(2,1)S(1)}, u32[]{:S(2)}, u32[]{:S(2)}) collective-permute-start(bf16[72,768]{1,0:T(8,128)(2,1)S(1)} %get-tuple-element.89), channel_id=1, source_target_pairs={{0,16},{4,20},{8,24},{12,28},{16,0},{20,4},{24,8},{28,12},{1,17},{... | collective-permute-start | bytes 331784 | tf_op jit(solution)/shard_map/ppermute | solution.py:16
  57.5 1.5 %collective-permute-start.31 = (bf16[72,768]{1,0:T(8,128)(2,1)S(1)}, bf16[72,768]{1,0:T(8,128)(2,1)S(1)}, u32[]{:S(2)}, u32[]{:S(2)}) collective-permute-start(bf16[72,768]{1,0:T(8,128)(2,1)S(1)} %get-tuple-element.90), channel_id=1, source_target_pairs={{0,24},{4,28},{8,16},{12,20},{16,8},{20,12},{24,0},{28,4},{1,25},{... | collective-permute-start | bytes 331784 | tf_op jit(solution)/shard_map/ppermute | solution.py:16
  59.0 0.7 collective-permute-done.29
  59.6 7.9 %collective-permute-done.30 = bf16[72,768]{1,0:T(8,128)(2,1)S(1)} collective-permute-done((bf16[72,768]{1,0:T(8,128)(2,1)S(1)}, bf16[72,768]{1,0:T(8,128)(2,1)S(1)}, u32[]{:S(2)}, u32[]{:S(2)}) %collective-permute-start.30) | collective-permute-done | bytes 110624 | tf_op jit(solution)/shard_map/ppermute | solution.py:16
  67.8 0.7 reshape.496
  68.5 0.6 pad_maximum_fusion.10
  69.1 0.7 %fusion.24 = bf16[64,768]{1,0:T(8,128)(2,1)} fusion(f32[1,4,64,768]{3,2,1,0:T(8,128)S(1)} %bitcast.67, s32[]{:T(128)S(6)} %select_n.199, bf16[72,768]{1,0:T(8,128)(2,1)S(1)} %collective-permute-done.31, bf16[72,768]{1,0:T(8,128)(2,1)S(1)} %collective-permute-done.30, bf16[72,768]{1,0:T(8,128)(2,1)S(1)} %collective-permute-done.29, f32[64]{0:T(128)S(1)} %fusion.58), kind=kLoop, calls=%fused_computation.116 | loop fusion | flops 393216 | bytes 590084 | tf_op jit(solution)/shard_map/convert_element_type | solution.py:240
  (80 shorter events, 1.6 us)
Async XLA Ops:
  0.6 11.2 %collective-permute-start.16 = (bf16[128,768]{1,0:T(8,128)(2,1)}, bf16[128,768]{1,0:T(8,128)(2,1)S(1)}, u32[]{:S(2)}, u32[]{:S(2)}) collective-permute-start(bf16[128,768]{1,0:T(8,128)(2,1)} %param.5), channel_id=1, source_target_pairs={{0,2},{1,3},{2,0},{3,1},{4,6},{5,7},{6,4},{7,5},{8,10},{9,11},{10,... | collective-permute-start | bytes 589832 | tf_op jit(solution)/shard_map/ppermute | solution.py:16
  3.7 8.1 %collective-permute-start.15 = (bf16[128,768]{1,0:T(8,128)(2,1)}, bf16[128,768]{1,0:T(8,128)(2,1)S(1)}, u32[]{:S(2)}, u32[]{:S(2)}) collective-permute-start(bf16[128,768]{1,0:T(8,128)(2,1)} %param.5), channel_id=1, source_target_pairs={{0,1},{1,0},{2,3},{3,2},{4,5},{5,4},{6,7},{7,6},{8,9},{9,8},{10,11... | collective-permute-start | bytes 589832 | tf_op jit(solution)/shard_map/ppermute | solution.py:16
  5.2 1.4 %collective-permute-start.19 = (s32[4,4]{1,0:T(4,128)}, s32[4,4]{1,0:T(4,128)S(1)}, u32[]{:S(2)}, u32[]{:S(2)}) collective-permute-start(s32[4,4]{1,0:T(4,128)} %param.7), channel_id=1, source_target_pairs={{0,4},{4,0},{8,12},{12,8},{16,20},{20,16},{24,28},{28,24},{1,5},{5... | collective-permute-start | bytes 200 | tf_op jit(solution)/shard_map/ppermute | solution.py:16
  6.5 12.4 %collective-permute-start.22 = (bf16[64,768]{1,0:T(8,128)(2,1)}, bf16[64,768]{1,0:T(8,128)(2,1)S(1)}, u32[]{:S(2)}, u32[]{:S(2)}) collective-permute-start(bf16[64,768]{1,0:T(8,128)(2,1)} %param.6), channel_id=1, source_target_pairs={{0,24},{4,28},{8,16},{12,20},{16,8},{20,12},{24,0},{28,4},{1,25},{... | collective-permute-start | bytes 294920 | tf_op jit(solution)/shard_map/ppermute | solution.py:16
  10.1 8.8 %collective-permute-start.21 = (bf16[64,768]{1,0:T(8,128)(2,1)}, bf16[64,768]{1,0:T(8,128)(2,1)S(1)}, u32[]{:S(2)}, u32[]{:S(2)}) collective-permute-start(bf16[64,768]{1,0:T(8,128)(2,1)} %param.6), channel_id=1, source_target_pairs={{0,16},{4,20},{8,24},{12,28},{16,0},{20,4},{24,8},{28,12},{1,17},{... | collective-permute-start | bytes 294920 | tf_op jit(solution)/shard_map/ppermute | solution.py:16
  10.1 8.8 %collective-permute-start.20 = (bf16[64,768]{1,0:T(8,128)(2,1)}, bf16[64,768]{1,0:T(8,128)(2,1)S(1)}, u32[]{:S(2)}, u32[]{:S(2)}) collective-permute-start(bf16[64,768]{1,0:T(8,128)(2,1)} %param.6), channel_id=1, source_target_pairs={{0,8},{4,12},{8,0},{12,4},{16,24},{20,28},{24,16},{28,20},{1,9},{5... | collective-permute-start | bytes 294920 | tf_op jit(solution)/shard_map/ppermute | solution.py:16
  12.8 6.1 %collective-permute-start.17 = (bf16[384,768]{1,0:T(8,128)(2,1)S(1)}, bf16[384,768]{1,0:T(8,128)(2,1)S(1)}, u32[]{:S(2)}, u32[]{:S(2)}) collective-permute-start(bf16[384,768]{1,0:T(8,128)(2,1)S(1)} %pad_maximum_fusion.6), channel_id=1, source_target_pairs={{0,4},{4,0},{8,12},{12,8},{16,20},{20,16},{24,28},{28,24},{1,5},{5... | collective-permute-start | bytes 1769480 | tf_op jit(solution)/shard_map/ppermute | solution.py:16
  13.2 5.7 %collective-permute-start.18 = (bf16[128,768]{1,0:T(8,128)(2,1)S(1)}, bf16[128,768]{1,0:T(8,128)(2,1)S(1)}, u32[]{:S(2)}, u32[]{:S(2)}) collective-permute-start(bf16[128,768]{1,0:T(8,128)(2,1)S(1)} %broadcast_select_fusion), channel_id=1, source_target_pairs={{0,2},{1,3},{2,0},{3,1},{4,5},{5,4},{6,7},{7,6},{8,10},{9,11},{10,... | collective-permute-start | bytes 589832 | tf_op jit(solution)/shard_map/ppermute | solution.py:23
  13.8 5.2 %copy-start.3 = (bf16[64,768]{1,0:T(8,128)(2,1)S(1)}, bf16[64,768]{1,0:T(8,128)(2,1)}, u32[]{:S(2)}) copy-start(bf16[64,768]{1,0:T(8,128)(2,1)} %param.6) | copy-start | bytes 294916
  13.8 6.3 %copy-start.2 = (bf16[128,768]{1,0:T(8,128)(2,1)S(1)}, bf16[128,768]{1,0:T(8,128)(2,1)}, u32[]{:S(2)}) copy-start(bf16[128,768]{1,0:T(8,128)(2,1)} %param.5) | copy-start | bytes 589828
  18.9 1.5 %collective-permute-start.27 = (bf16[128,768]{1,0:T(8,128)(2,1)S(1)}, bf16[128,768]{1,0:T(8,128)(2,1)S(1)}, u32[]{:S(2)}, u32[]{:S(2)}) collective-permute-start(bf16[128,768]{1,0:T(8,128)(2,1)S(1)} %collective-permute-done.18), channel_id=1, source_target_pairs={{0,4},{4,0},{8,12},{12,8},{16,20},{20,16},{24,28},{28,24},{1,5},{5... | collective-permute-start | bytes 589832 | tf_op jit(solution)/shard_map/ppermute | solution.py:16
  19.0 1.5 %collective-permute-start.23 = (bf16[64,768]{1,0:T(8,128)(2,1)S(1)}, bf16[64,768]{1,0:T(8,128)(2,1)S(1)}, u32[]{:S(2)}, u32[]{:S(2)}) collective-permute-start(bf16[64,768]{1,0:T(8,128)(2,1)S(1)} %copy-done.3), channel_id=1, source_target_pairs={{0,4},{4,0},{8,12},{12,8},{16,20},{20,16},{24,28},{28,24},{1,5},{5... | collective-permute-start | bytes 294920 | tf_op jit(solution)/shard_map/ppermute | solution.py:16
  19.6 1.3 %collective-permute-start.24 = (bf16[64,768]{1,0:T(8,128)(2,1)S(1)}, bf16[64,768]{1,0:T(8,128)(2,1)S(1)}, u32[]{:S(2)}, u32[]{:S(2)}) collective-permute-start(bf16[64,768]{1,0:T(8,128)(2,1)S(1)} %collective-permute-done.20), channel_id=1, source_target_pairs={{0,4},{4,0},{8,12},{12,8},{16,20},{20,16},{24,28},{28,24},{1,5},{5... | collective-permute-start | bytes 294920 | tf_op jit(solution)/shard_map/ppermute | solution.py:16
  19.6 1.4 %collective-permute-start.25 = (bf16[64,768]{1,0:T(8,128)(2,1)S(1)}, bf16[64,768]{1,0:T(8,128)(2,1)S(1)}, u32[]{:S(2)}, u32[]{:S(2)}) collective-permute-start(bf16[64,768]{1,0:T(8,128)(2,1)S(1)} %collective-permute-done.21), channel_id=1, source_target_pairs={{0,4},{4,0},{8,12},{12,8},{16,20},{20,16},{24,28},{28,24},{1,5},{5... | collective-permute-start | bytes 294920 | tf_op jit(solution)/shard_map/ppermute | solution.py:16
  20.1 1.3 %collective-permute-start.26 = (bf16[64,768]{1,0:T(8,128)(2,1)S(1)}, bf16[64,768]{1,0:T(8,128)(2,1)S(1)}, u32[]{:S(2)}, u32[]{:S(2)}) collective-permute-start(bf16[64,768]{1,0:T(8,128)(2,1)S(1)} %collective-permute-done.22), channel_id=1, source_target_pairs={{0,4},{4,0},{8,12},{12,8},{16,20},{20,16},{24,28},{28,24},{1,5},{5... | collective-permute-start | bytes 294920 | tf_op jit(solution)/shard_map/ppermute | solution.py:16
  20.4 1.0 %copy-start = (bf16[512,768]{1,0:T(8,128)(2,1)}, bf16[512,768]{1,0:T(8,128)(2,1)S(1)}, u32[]{:S(2)}) copy-start(bf16[512,768]{1,0:T(8,128)(2,1)S(1)} %constant_dynamic-update-slice_fusion.48) | copy-start | bytes 2359300
  22.7 29.4 %collective-permute-start.28 = (f32[3,512]{1,0:T(4,128)S(1)}, f32[3,512]{1,0:T(4,128)S(1)}, u32[]{:S(2)}, u32[]{:S(2)}) collective-permute-start(f32[3,512]{1,0:T(4,128)S(1)} %get-tuple-element.102), channel_id=1, source_target_pairs={{0,4},{4,0},{8,12},{12,8},{16,20},{20,16},{24,28},{28,24},{1,5},{5... | collective-permute-start | bytes 18440 | tf_op jit(solution)/shard_map/ppermute | solution.py:16
  52.2 1.1 %copy-start.1 = (bf16[512,768]{1,0:T(8,128)(2,1)S(1)}, bf16[512,768]{1,0:T(8,128)(2,1)}, u32[]{:S(2)}) copy-start(bf16[512,768]{1,0:T(8,128)(2,1)} %copy-done) | copy-start | bytes 2359300
  54.3 5.4 %collective-permute-start.29 = (bf16[72,768]{1,0:T(8,128)(2,1)S(1)}, bf16[72,768]{1,0:T(8,128)(2,1)S(1)}, u32[]{:S(2)}, u32[]{:S(2)}) collective-permute-start(bf16[72,768]{1,0:T(8,128)(2,1)S(1)} %get-tuple-element.88), channel_id=1, source_target_pairs={{0,8},{4,12},{8,0},{12,4},{16,24},{20,28},{24,16},{28,20},{1,9},{5... | collective-permute-start | bytes 331784 | tf_op jit(solution)/shard_map/ppermute | solution.py:16
  56.3 11.3 %collective-permute-start.30 = (bf16[72,768]{1,0:T(8,128)(2,1)S(1)}, bf16[72,768]{1,0:T(8,128)(2,1)S(1)}, u32[]{:S(2)}, u32[]{:S(2)}) collective-permute-start(bf16[72,768]{1,0:T(8,128)(2,1)S(1)} %get-tuple-element.89), channel_id=1, source_target_pairs={{0,16},{4,20},{8,24},{12,28},{16,0},{20,4},{24,8},{28,12},{1,17},{... | collective-permute-start | bytes 331784 | tf_op jit(solution)/shard_map/ppermute | solution.py:16
  57.5 10.1 %collective-permute-start.31 = (bf16[72,768]{1,0:T(8,128)(2,1)S(1)}, bf16[72,768]{1,0:T(8,128)(2,1)S(1)}, u32[]{:S(2)}, u32[]{:S(2)}) collective-permute-start(bf16[72,768]{1,0:T(8,128)(2,1)S(1)} %get-tuple-element.90), channel_id=1, source_target_pairs={{0,24},{4,28},{8,16},{12,20},{16,8},{20,12},{24,0},{28,4},{1,25},{... | collective-permute-start | bytes 331784 | tf_op jit(solution)/shard_map/ppermute | solution.py:16
where the time goes:
time: 70 us; the launch traced here: 69.8 us
  starting transfers between devices  43.7 us (62%)
  waiting for transfers between devices  16.4 us (23%)
  other arithmetic  3.85 us (6%)
  matrix products  2.57 us (4%)
  local copies, waits for them, and re-layouts  2.15 us (3%)
  between operations  1.07 us (2%)
    ppermute x16, starting transfers between devices, swap(): lax.ppermute(x, axis, [(i, i ^ k) for i in range(lax.axis_size(axis))])  43.2 us
    ppermute x16, waiting for transfers between devices, swap(): lax.ppermute(x, axis, [(i, i ^ k) for i in range(lax.axis_size(axis))])  11.6 us
    ppermute x1, waiting for transfers between devices, swap_by_core(): return lax.ppermute(x, ('row', 'col'), pairs)  4.83 us
  transfers between devices with their start and end apart: 17, of which 9 were waited for; matrix products, arithmetic and copies ran while one was open for 4% of the time, Pallas kernels for 0%

commit v1 on v0

--- a/solution.py
+++ b/solution.py
@@ -226,10 +226,12 @@
         parts, masses = [lax.dynamic_index_in_dim(held, me, 1, keepdims=False)], [from_thirds(note, group_cols)]
         for d in range(1, size):
             block = lax.dynamic_index_in_dim(low, me ^ d, 1, keepdims=False).reshape(-1, width)
-            got = swap(jnp.concatenate([block, note]), "row", d << at)
-            if d << at == 2:
-                row_out = after(row_pot[:row_count], got)
+            message = jnp.concatenate([block, note])
+            if at == 1 and d == size - 1:
+                row_out = after(row_pot[:row_count], low)
                 row_out = jnp.concatenate(unxor_list(jnp.split(row_out, cols), me_col))
+                message, row_out = lax.optimization_barrier((message, row_out))
+            got = swap(message, "row", d << at)
             parts.append(got[: block.shape[0]].astype(jnp.float32).reshape(parts[0].shape))
             masses.append(from_thirds(got[block.shape[0] :], group_cols))
         held, mass = add(parts), add(masses)

time: 70 us -> 70.4 us (level)
  transfers between devices with their start and end apart: 17 -> 17, of which waited for: 9 -> 10; matrix products, arithmetic and copies ran while one was open for 4% -> 4% of each run, Pallas kernels for 0% -> 0%
where the time goes in v1:
time: 70.4 us; the launch traced here: 70.2 us
  starting transfers between devices  43.7 us (62%)
  waiting for transfers between devices  16.8 us (24%)
  other arithmetic  3.86 us (5%)
  matrix products  2.57 us (4%)
  local copies, waits for them, and re-layouts  2.18 us (3%)
  between operations  1.06 us (2%)
    ppermute x16, starting transfers between devices, swap(): lax.ppermute(x, axis, [(i, i ^ k) for i in range(lax.axis_size(axis))])  43.2 us
    ppermute x16, waiting for transfers between devices, swap(): lax.ppermute(x, axis, [(i, i ^ k) for i in range(lax.axis_size(axis))])  11.9 us
    ppermute x1, waiting for transfers between devices, swap_by_core(): return lax.ppermute(x, ('row', 'col'), pairs)  4.83 us
  transfers between devices with their start and end apart: 17, of which 10 were waited for; matrix products, arithmetic and copies ran while one was open for 4% of the time, Pallas kernels for 0%

profile of v1, /device:TPU:0, one launch (start us, length us, event | category | flops | bytes accessed | tf_op | source)
XLA Modules:
  0.0 70.2 jit_solution(8964890004658965275)
XLA Ops:
  0.6 3.0 %collective-permute-start.16 = (bf16[128,768]{1,0:T(8,128)(2,1)}, bf16[128,768]{1,0:T(8,128)(2,1)S(1)}, u32[]{:S(2)}, u32[]{:S(2)}) collective-permute-start(bf16[128,768]{1,0:T(8,128)(2,1)} %param.5), channel_id=1, source_target_pairs={{0,2},{1,3},{2,0},{3,1},{4,6},{5,7},{6,4},{7,5},{8,10},{9,11},{10,... | collective-permute-start | bytes 589832 | tf_op jit(solution)/shard_map/ppermute | solution.py:16
  3.7 1.5 %collective-permute-start.15 = (bf16[128,768]{1,0:T(8,128)(2,1)}, bf16[128,768]{1,0:T(8,128)(2,1)S(1)}, u32[]{:S(2)}, u32[]{:S(2)}) collective-permute-start(bf16[128,768]{1,0:T(8,128)(2,1)} %param.5), channel_id=1, source_target_pairs={{0,1},{1,0},{2,3},{3,2},{4,5},{5,4},{6,7},{7,6},{8,9},{9,8},{10,11... | collective-permute-start | bytes 589832 | tf_op jit(solution)/shard_map/ppermute | solution.py:16
  5.2 1.3 %collective-permute-done.19 = s32[4,4]{1,0:T(4,128)S(1)} collective-permute-done((s32[4,4]{1,0:T(4,128)}, s32[4,4]{1,0:T(4,128)S(1)}, u32[]{:S(2)}, u32[]{:S(2)}) %collective-permute-start.19) | collective-permute-done | bytes 96 | tf_op jit(solution)/shard_map/ppermute | solution.py:16
  6.5 3.6 %collective-permute-start.22 = (bf16[64,768]{1,0:T(8,128)(2,1)}, bf16[64,768]{1,0:T(8,128)(2,1)S(1)}, u32[]{:S(2)}, u32[]{:S(2)}) collective-permute-start(bf16[64,768]{1,0:T(8,128)(2,1)} %param.6), channel_id=1, source_target_pairs={{0,24},{4,28},{8,16},{12,20},{16,8},{20,12},{24,0},{28,4},{1,25},{... | collective-permute-start | bytes 294920 | tf_op jit(solution)/shard_map/ppermute | solution.py:16
  10.1 0.8 %collective-permute-start.20 = (bf16[64,768]{1,0:T(8,128)(2,1)}, bf16[64,768]{1,0:T(8,128)(2,1)S(1)}, u32[]{:S(2)}, u32[]{:S(2)}) collective-permute-start(bf16[64,768]{1,0:T(8,128)(2,1)} %param.6), channel_id=1, source_target_pairs={{0,8},{4,12},{8,0},{12,4},{16,24},{20,28},{24,16},{28,20},{1,9},{5... | collective-permute-start | bytes 294920 | tf_op jit(solution)/shard_map/ppermute | solution.py:16
  10.9 0.8 %compare_reduce_fusion = (pred[4,4]{1,0:T(4,128)(4,1)S(1)}, pred[4,4]{1,0:T(4,128)(4,1)S(1)}) fusion(s32[4,4]{1,0:T(4,128)S(1)} %collective-permute-done.19, s32[4]{0:T(128)S(1)} %iota_add_fusion, s32[4,4]{1,0:T(4,128)} %param.7), kind=kLoop, calls=%fused_computation.139 | loop fusion | flops 224 | bytes 176 | tf_op jit(solution)/shard_map/reduce_or | solution.py:166
  11.8 1.0 %pad_maximum_fusion.6 = bf16[384,768]{1,0:T(8,128)(2,1)S(1)} fusion(bf16[128,768]{1,0:T(8,128)(2,1)S(1)} %collective-permute-done.16, bf16[128,768]{1,0:T(8,128)(2,1)S(1)} %collective-permute-done.15, bf16[128,768]{1,0:T(8,128)(2,1)} %param.5), kind=kLoop, calls=%fused_computation.99 | loop fusion | flops 1769472 | bytes 1179648 | tf_op jit(solution)/shard_map/concatenate | solution.py:48
  12.9 0.3 convolution_compare_fusion.1
  13.2 0.6 collective-permute-start.18
  13.8 0.3 convolution_compare_fusion
  14.1 4.8 %collective-permute-done.18 = bf16[128,768]{1,0:T(8,128)(2,1)S(1)} collective-permute-done((bf16[128,768]{1,0:T(8,128)(2,1)S(1)}, bf16[128,768]{1,0:T(8,128)(2,1)S(1)}, u32[]{:S(2)}, u32[]{:S(2)}) %collective-permute-start.18) | collective-permute-done | bytes 196640 | tf_op jit(solution)/shard_map/ppermute | solution.py:23
  19.0 0.6 collective-permute-start.23
  19.6 0.4 collective-permute-start.25
  20.6 0.3 collective-permute-done.24
  20.9 0.1 collective-permute-done.25
  21.0 0.3 collective-permute-done.26
  21.4 0.6 fusion.10
  22.0 0.6 fusion.11
  22.7 28.6 %collective-permute-start.28 = (f32[3,512]{1,0:T(4,128)S(1)}, f32[3,512]{1,0:T(4,128)S(1)}, u32[]{:S(2)}, u32[]{:S(2)}) collective-permute-start(f32[3,512]{1,0:T(4,128)S(1)} %get-tuple-element.106), channel_id=1, source_target_pairs={{0,4},{4,0},{8,12},{12,8},{16,20},{20,16},{24,28},{28,24},{1,5},{5... | collective-permute-start | bytes 18440 | tf_op jit(solution)/shard_map/ppermute | solution.py:16
  51.2 0.8 %collective-permute-done.28 = f32[3,512]{1,0:T(4,128)S(1)} collective-permute-done((f32[3,512]{1,0:T(4,128)S(1)}, f32[3,512]{1,0:T(4,128)S(1)}, u32[]{:S(2)}, u32[]{:S(2)}) %collective-permute-start.28) | collective-permute-done | bytes 6176 | tf_op jit(solution)/shard_map/ppermute | solution.py:16
  52.2 0.4 exponential_reduce_fusion.10
  52.6 0.7 copy-done.1
  53.3 0.4 fusion.16
  53.7 0.4 convolution_add_fusion
  54.3 0.6 pad_maximum_fusion.10
  54.9 2.4 %collective-permute-start.31 = (bf16[72,768]{1,0:T(8,128)(2,1)S(1)}, bf16[72,768]{1,0:T(8,128)(2,1)S(1)}, u32[]{:S(2)}, u32[]{:S(2)}) collective-permute-start(bf16[72,768]{1,0:T(8,128)(2,1)S(1)} %get-tuple-element.34), channel_id=1, source_target_pairs={{0,24},{4,28},{8,16},{12,20},{16,8},{20,12},{24,0},{28,4},{1,25},{... | collective-permute-start | bytes 331784 | tf_op jit(solution)/shard_map/ppermute | solution.py:16
  57.5 2.0 %collective-permute-start.30 = (bf16[72,768]{1,0:T(8,128)(2,1)S(1)}, bf16[72,768]{1,0:T(8,128)(2,1)S(1)}, u32[]{:S(2)}, u32[]{:S(2)}) collective-permute-start(bf16[72,768]{1,0:T(8,128)(2,1)S(1)} %get-tuple-element.93), channel_id=1, source_target_pairs={{0,16},{4,20},{8,24},{12,28},{16,0},{20,4},{24,8},{28,12},{1,17},{... | collective-permute-start | bytes 331784 | tf_op jit(solution)/shard_map/ppermute | solution.py:16
  59.6 3.1 %collective-permute-done.31 = bf16[72,768]{1,0:T(8,128)(2,1)S(1)} collective-permute-done((bf16[72,768]{1,0:T(8,128)(2,1)S(1)}, bf16[72,768]{1,0:T(8,128)(2,1)S(1)}, u32[]{:S(2)}, u32[]{:S(2)}) %collective-permute-start.31) | collective-permute-done | bytes 110624 | tf_op jit(solution)/shard_map/ppermute | solution.py:16
  62.7 2.6 %collective-permute-done.29 = bf16[72,768]{1,0:T(8,128)(2,1)S(1)} collective-permute-done((bf16[72,768]{1,0:T(8,128)(2,1)S(1)}, bf16[72,768]{1,0:T(8,128)(2,1)S(1)}, u32[]{:S(2)}, u32[]{:S(2)}) %collective-permute-start.29) | collective-permute-done | bytes 110624 | tf_op jit(solution)/shard_map/ppermute | solution.py:16
  65.3 3.2 %collective-permute-done.30 = bf16[72,768]{1,0:T(8,128)(2,1)S(1)} collective-permute-done((bf16[72,768]{1,0:T(8,128)(2,1)S(1)}, bf16[72,768]{1,0:T(8,128)(2,1)S(1)}, u32[]{:S(2)}, u32[]{:S(2)}) %collective-permute-start.30) | collective-permute-done | bytes 110624 | tf_op jit(solution)/shard_map/ppermute | solution.py:16
  68.7 0.7 reshape.496
  69.5 0.7 %fusion.24 = bf16[64,768]{1,0:T(8,128)(2,1)} fusion(f32[1,4,64,768]{3,2,1,0:T(8,128)S(1)} %bitcast.67, s32[]{:T(128)S(6)} %select_n.199, bf16[72,768]{1,0:T(8,128)(2,1)S(1)} %collective-permute-done.31, bf16[72,768]{1,0:T(8,128)(2,1)S(1)} %collective-permute-done.30, bf16[72,768]{1,0:T(8,128)(2,1)S(1)} %collective-permute-done.29, f32[64]{0:T(128)S(1)} %fusion.58), kind=kLoop, calls=%fused_computation.116 | loop fusion | flops 393216 | bytes 590084 | tf_op jit(solution)/shard_map/convert_element_type | solution.py:242
  (80 shorter events, 1.6 us)
Async XLA Ops:
  0.6 11.2 %collective-permute-start.16 = (bf16[128,768]{1,0:T(8,128)(2,1)}, bf16[128,768]{1,0:T(8,128)(2,1)S(1)}, u32[]{:S(2)}, u32[]{:S(2)}) collective-permute-start(bf16[128,768]{1,0:T(8,128)(2,1)} %param.5), channel_id=1, source_target_pairs={{0,2},{1,3},{2,0},{3,1},{4,6},{5,7},{6,4},{7,5},{8,10},{9,11},{10,... | collective-permute-start | bytes 589832 | tf_op jit(solution)/shard_map/ppermute | solution.py:16
  3.7 8.1 %collective-permute-start.15 = (bf16[128,768]{1,0:T(8,128)(2,1)}, bf16[128,768]{1,0:T(8,128)(2,1)S(1)}, u32[]{:S(2)}, u32[]{:S(2)}) collective-permute-start(bf16[128,768]{1,0:T(8,128)(2,1)} %param.5), channel_id=1, source_target_pairs={{0,1},{1,0},{2,3},{3,2},{4,5},{5,4},{6,7},{7,6},{8,9},{9,8},{10,11... | collective-permute-start | bytes 589832 | tf_op jit(solution)/shard_map/ppermute | solution.py:16
  5.2 1.4 %collective-permute-start.19 = (s32[4,4]{1,0:T(4,128)}, s32[4,4]{1,0:T(4,128)S(1)}, u32[]{:S(2)}, u32[]{:S(2)}) collective-permute-start(s32[4,4]{1,0:T(4,128)} %param.7), channel_id=1, source_target_pairs={{0,4},{4,0},{8,12},{12,8},{16,20},{20,16},{24,28},{28,24},{1,5},{5... | collective-permute-start | bytes 200 | tf_op jit(solution)/shard_map/ppermute | solution.py:16
  6.5 12.4 %collective-permute-start.22 = (bf16[64,768]{1,0:T(8,128)(2,1)}, bf16[64,768]{1,0:T(8,128)(2,1)S(1)}, u32[]{:S(2)}, u32[]{:S(2)}) collective-permute-start(bf16[64,768]{1,0:T(8,128)(2,1)} %param.6), channel_id=1, source_target_pairs={{0,24},{4,28},{8,16},{12,20},{16,8},{20,12},{24,0},{28,4},{1,25},{... | collective-permute-start | bytes 294920 | tf_op jit(solution)/shard_map/ppermute | solution.py:16
  10.1 8.8 %collective-permute-start.21 = (bf16[64,768]{1,0:T(8,128)(2,1)}, bf16[64,768]{1,0:T(8,128)(2,1)S(1)}, u32[]{:S(2)}, u32[]{:S(2)}) collective-permute-start(bf16[64,768]{1,0:T(8,128)(2,1)} %param.6), channel_id=1, source_target_pairs={{0,16},{4,20},{8,24},{12,28},{16,0},{20,4},{24,8},{28,12},{1,17},{... | collective-permute-start | bytes 294920 | tf_op jit(solution)/shard_map/ppermute | solution.py:16
  10.1 8.8 %collective-permute-start.20 = (bf16[64,768]{1,0:T(8,128)(2,1)}, bf16[64,768]{1,0:T(8,128)(2,1)S(1)}, u32[]{:S(2)}, u32[]{:S(2)}) collective-permute-start(bf16[64,768]{1,0:T(8,128)(2,1)} %param.6), channel_id=1, source_target_pairs={{0,8},{4,12},{8,0},{12,4},{16,24},{20,28},{24,16},{28,20},{1,9},{5... | collective-permute-start | bytes 294920 | tf_op jit(solution)/shard_map/ppermute | solution.py:16
  12.8 6.1 %collective-permute-start.17 = (bf16[384,768]{1,0:T(8,128)(2,1)S(1)}, bf16[384,768]{1,0:T(8,128)(2,1)S(1)}, u32[]{:S(2)}, u32[]{:S(2)}) collective-permute-start(bf16[384,768]{1,0:T(8,128)(2,1)S(1)} %pad_maximum_fusion.6), channel_id=1, source_target_pairs={{0,4},{4,0},{8,12},{12,8},{16,20},{20,16},{24,28},{28,24},{1,5},{5... | collective-permute-start | bytes 1769480 | tf_op jit(solution)/shard_map/ppermute | solution.py:16
  13.2 5.7 %collective-permute-start.18 = (bf16[128,768]{1,0:T(8,128)(2,1)S(1)}, bf16[128,768]{1,0:T(8,128)(2,1)S(1)}, u32[]{:S(2)}, u32[]{:S(2)}) collective-permute-start(bf16[128,768]{1,0:T(8,128)(2,1)S(1)} %broadcast_select_fusion), channel_id=1, source_target_pairs={{0,2},{1,3},{2,0},{3,1},{4,5},{5,4},{6,7},{7,6},{8,10},{9,11},{10,... | collective-permute-start | bytes 589832 | tf_op jit(solution)/shard_map/ppermute | solution.py:23
  13.8 5.2 %copy-start.3 = (bf16[64,768]{1,0:T(8,128)(2,1)S(1)}, bf16[64,768]{1,0:T(8,128)(2,1)}, u32[]{:S(2)}) copy-start(bf16[64,768]{1,0:T(8,128)(2,1)} %param.6) | copy-start | bytes 294916
  13.8 6.3 %copy-start.2 = (bf16[128,768]{1,0:T(8,128)(2,1)S(1)}, bf16[128,768]{1,0:T(8,128)(2,1)}, u32[]{:S(2)}) copy-start(bf16[128,768]{1,0:T(8,128)(2,1)} %param.5) | copy-start | bytes 589828
  18.9 1.5 %collective-permute-start.27 = (bf16[128,768]{1,0:T(8,128)(2,1)S(1)}, bf16[128,768]{1,0:T(8,128)(2,1)S(1)}, u32[]{:S(2)}, u32[]{:S(2)}) collective-permute-start(bf16[128,768]{1,0:T(8,128)(2,1)S(1)} %collective-permute-done.18), channel_id=1, source_target_pairs={{0,4},{4,0},{8,12},{12,8},{16,20},{20,16},{24,28},{28,24},{1,5},{5... | collective-permute-start | bytes 589832 | tf_op jit(solution)/shard_map/ppermute | solution.py:16
  19.0 1.5 %collective-permute-start.23 = (bf16[64,768]{1,0:T(8,128)(2,1)S(1)}, bf16[64,768]{1,0:T(8,128)(2,1)S(1)}, u32[]{:S(2)}, u32[]{:S(2)}) collective-permute-start(bf16[64,768]{1,0:T(8,128)(2,1)S(1)} %copy-done.3), channel_id=1, source_target_pairs={{0,4},{4,0},{8,12},{12,8},{16,20},{20,16},{24,28},{28,24},{1,5},{5... | collective-permute-start | bytes 294920 | tf_op jit(solution)/shard_map/ppermute | solution.py:16
  19.6 1.3 %collective-permute-start.24 = (bf16[64,768]{1,0:T(8,128)(2,1)S(1)}, bf16[64,768]{1,0:T(8,128)(2,1)S(1)}, u32[]{:S(2)}, u32[]{:S(2)}) collective-permute-start(bf16[64,768]{1,0:T(8,128)(2,1)S(1)} %collective-permute-done.20), channel_id=1, source_target_pairs={{0,4},{4,0},{8,12},{12,8},{16,20},{20,16},{24,28},{28,24},{1,5},{5... | collective-permute-start | bytes 294920 | tf_op jit(solution)/shard_map/ppermute | solution.py:16
  19.6 1.4 %collective-permute-start.25 = (bf16[64,768]{1,0:T(8,128)(2,1)S(1)}, bf16[64,768]{1,0:T(8,128)(2,1)S(1)}, u32[]{:S(2)}, u32[]{:S(2)}) collective-permute-start(bf16[64,768]{1,0:T(8,128)(2,1)S(1)} %collective-permute-done.21), channel_id=1, source_target_pairs={{0,4},{4,0},{8,12},{12,8},{16,20},{20,16},{24,28},{28,24},{1,5},{5... | collective-permute-start | bytes 294920 | tf_op jit(solution)/shard_map/ppermute | solution.py:16
  20.1 1.3 %collective-permute-start.26 = (bf16[64,768]{1,0:T(8,128)(2,1)S(1)}, bf16[64,768]{1,0:T(8,128)(2,1)S(1)}, u32[]{:S(2)}, u32[]{:S(2)}) collective-permute-start(bf16[64,768]{1,0:T(8,128)(2,1)S(1)} %collective-permute-done.22), channel_id=1, source_target_pairs={{0,4},{4,0},{8,12},{12,8},{16,20},{20,16},{24,28},{28,24},{1,5},{5... | collective-permute-start | bytes 294920 | tf_op jit(solution)/shard_map/ppermute | solution.py:16
  20.4 1.0 %copy-start = (bf16[512,768]{1,0:T(8,128)(2,1)}, bf16[512,768]{1,0:T(8,128)(2,1)S(1)}, u32[]{:S(2)}) copy-start(bf16[512,768]{1,0:T(8,128)(2,1)S(1)} %constant_dynamic-update-slice_fusion.48) | copy-start | bytes 2359300
  22.7 29.4 %collective-permute-start.28 = (f32[3,512]{1,0:T(4,128)S(1)}, f32[3,512]{1,0:T(4,128)S(1)}, u32[]{:S(2)}, u32[]{:S(2)}) collective-permute-start(f32[3,512]{1,0:T(4,128)S(1)} %get-tuple-element.106), channel_id=1, source_target_pairs={{0,4},{4,0},{8,12},{12,8},{16,20},{20,16},{24,28},{28,24},{1,5},{5... | collective-permute-start | bytes 18440 | tf_op jit(solution)/shard_map/ppermute | solution.py:16
  52.2 1.1 %copy-start.1 = (bf16[512,768]{1,0:T(8,128)(2,1)S(1)}, bf16[512,768]{1,0:T(8,128)(2,1)}, u32[]{:S(2)}) copy-start(bf16[512,768]{1,0:T(8,128)(2,1)} %copy-done) | copy-start | bytes 2359300
  54.9 7.8 %collective-permute-start.31 = (bf16[72,768]{1,0:T(8,128)(2,1)S(1)}, bf16[72,768]{1,0:T(8,128)(2,1)S(1)}, u32[]{:S(2)}, u32[]{:S(2)}) collective-permute-start(bf16[72,768]{1,0:T(8,128)(2,1)S(1)} %get-tuple-element.34), channel_id=1, source_target_pairs={{0,24},{4,28},{8,16},{12,20},{16,8},{20,12},{24,0},{28,4},{1,25},{... | collective-permute-start | bytes 331784 | tf_op jit(solution)/shard_map/ppermute | solution.py:16
  57.5 7.8 %collective-permute-start.29 = (bf16[72,768]{1,0:T(8,128)(2,1)S(1)}, bf16[72,768]{1,0:T(8,128)(2,1)S(1)}, u32[]{:S(2)}, u32[]{:S(2)}) collective-permute-start(bf16[72,768]{1,0:T(8,128)(2,1)S(1)} %get-tuple-element.92), channel_id=1, source_target_pairs={{0,8},{4,12},{8,0},{12,4},{16,24},{20,28},{24,16},{28,20},{1,9},{5... | collective-permute-start | bytes 331784 | tf_op jit(solution)/shard_map/ppermute | solution.py:16
  57.5 11.0 %collective-permute-start.30 = (bf16[72,768]{1,0:T(8,128)(2,1)S(1)}, bf16[72,768]{1,0:T(8,128)(2,1)S(1)}, u32[]{:S(2)}, u32[]{:S(2)}) collective-permute-start(bf16[72,768]{1,0:T(8,128)(2,1)S(1)} %get-tuple-element.93), channel_id=1, source_target_pairs={{0,16},{4,20},{8,24},{12,28},{16,0},{20,4},{24,8},{28,12},{1,17},{... | collective-permute-start | bytes 331784 | tf_op jit(solution)/shard_map/ppermute | solution.py:16

commit v2 on v0

--- a/solution.py
+++ b/solution.py
@@ -45,7 +45,8 @@
             near = lax.optimization_barrier((parts, passed_on))[0]
             ready = passed_on
             parts = parts + [swap_by_core(passed_on, "col", (2 << at, 1 << at))]
-    mate = [swap(part, "row", 1) for part in [jnp.concatenate(near)] + parts[3:]]
+    got = swap(jnp.concatenate(near[1:]), "row", 1)
+    mate = [swap(after(near[0], got), "row", 1), got] + [swap(part, "row", 1) for part in parts[3:]]
     return parts, mate, ready
 
 
@@ -154,8 +155,8 @@
 
     mate_pattern = swap(pattern, "row", 1)
     own_parts, mate_parts, ready = gather_spans(spans, core)
-    tile_centroids = gather_centroids(centroids, mate_pattern, mate_parts[0])
-    own_parts = [after(own_parts[0], mate_parts[0])] + own_parts[1:]
+    tile_centroids = gather_centroids(centroids, mate_pattern, mate_parts[1])
+    own_parts = [after(own_parts[0], mate_parts[1])] + own_parts[1:]
     span_halves = [jnp.concatenate(own_parts), jnp.concatenate(mate_parts)]
     at = jnp.arange(group_cols)
     row_of = at % half_cols // per * 2 + (at // half_cols ^ core)

time: 70 us -> 69.8 us (level)
  other arithmetic: 3.85 us -> 2.91 us
    concatenate x1, other arithmetic: 0.97 us -> 0.03 us  [gather_spans(): got = swap(jnp.concatenate(near[1:]), 'row', 1)]
    ppermute x16 -> x17, waiting for transfers between devices: 11.6 us -> 12 us  [swap(): lax.ppermute(x, axis, [(i, i ^ k) for i in range(lax.axis_size(axis))])]
    ppermute x16 -> x17, starting transfers between devices: 43.2 us -> 43.2 us  [swap(): lax.ppermute(x, axis, [(i, i ^ k) for i in range(lax.axis_size(axis))])]
  transfers between devices with their start and end apart: 17 -> 18, of which waited for: 9 -> 10; matrix products, arithmetic and copies ran while one was open for 4% -> 4% of each run, Pallas kernels for 0% -> 0%
where the time goes in v2:
time: 69.8 us; the launch traced here: 69.6 us
  starting transfers between devices  43.8 us (63%)
  waiting for transfers between devices  16.8 us (24%)
  other arithmetic  2.91 us (4%)
  matrix products  2.56 us (4%)
  local copies, waits for them, and re-layouts  2.47 us (4%)
  between operations  1.05 us (2%)
    ppermute x17, starting transfers between devices, swap(): lax.ppermute(x, axis, [(i, i ^ k) for i in range(lax.axis_size(axis))])  43.2 us
    ppermute x17, waiting for transfers between devices, swap(): lax.ppermute(x, axis, [(i, i ^ k) for i in range(lax.axis_size(axis))])  12 us
    ppermute x1, waiting for transfers between devices, swap_by_core(): return lax.ppermute(x, ('row', 'col'), pairs)  4.83 us
  transfers between devices with their start and end apart: 18, of which 10 were waited for; matrix products, arithmetic and copies ran while one was open for 4% of the time, Pallas kernels for 0%

profile of v2, /device:TPU:0, one launch (start us, length us, event | category | flops | bytes accessed | tf_op | source)
XLA Modules:
  0.0 69.6 jit_solution(4479258535654220538)
XLA Ops:
  0.6 3.0 %collective-permute-start.15 = (bf16[128,768]{1,0:T(8,128)(2,1)}, bf16[128,768]{1,0:T(8,128)(2,1)S(1)}, u32[]{:S(2)}, u32[]{:S(2)}) collective-permute-start(bf16[128,768]{1,0:T(8,128)(2,1)} %param.5), channel_id=1, source_target_pairs={{0,1},{1,0},{2,3},{3,2},{4,5},{5,4},{6,7},{7,6},{8,9},{9,8},{10,11... | collective-permute-start | bytes 589832 | tf_op jit(solution)/shard_map/ppermute | solution.py:16
  3.6 1.5 %collective-permute-start.16 = (bf16[128,768]{1,0:T(8,128)(2,1)}, bf16[128,768]{1,0:T(8,128)(2,1)S(1)}, u32[]{:S(2)}, u32[]{:S(2)}) collective-permute-start(bf16[128,768]{1,0:T(8,128)(2,1)} %param.5), channel_id=1, source_target_pairs={{0,2},{1,3},{2,0},{3,1},{4,6},{5,7},{6,4},{7,5},{8,10},{9,11},{10,... | collective-permute-start | bytes 589832 | tf_op jit(solution)/shard_map/ppermute | solution.py:16
  5.2 1.3 %collective-permute-done.19 = s32[4,4]{1,0:T(4,128)S(1)} collective-permute-done((s32[4,4]{1,0:T(4,128)}, s32[4,4]{1,0:T(4,128)S(1)}, u32[]{:S(2)}, u32[]{:S(2)}) %collective-permute-start.19) | collective-permute-done | bytes 96 | tf_op jit(solution)/shard_map/ppermute | solution.py:16
  6.5 1.6 %collective-permute-start.20 = (bf16[64,768]{1,0:T(8,128)(2,1)}, bf16[64,768]{1,0:T(8,128)(2,1)S(1)}, u32[]{:S(2)}, u32[]{:S(2)}) collective-permute-start(bf16[64,768]{1,0:T(8,128)(2,1)} %param.6), channel_id=1, source_target_pairs={{0,8},{4,12},{8,0},{12,4},{16,24},{20,28},{24,16},{28,20},{1,9},{5... | collective-permute-start | bytes 294920 | tf_op jit(solution)/shard_map/ppermute | solution.py:16
  8.1 2.6 %collective-permute-start.21 = (bf16[64,768]{1,0:T(8,128)(2,1)}, bf16[64,768]{1,0:T(8,128)(2,1)S(1)}, u32[]{:S(2)}, u32[]{:S(2)}) collective-permute-start(bf16[64,768]{1,0:T(8,128)(2,1)} %param.6), channel_id=1, source_target_pairs={{0,16},{4,20},{8,24},{12,28},{16,0},{20,4},{24,8},{28,12},{1,17},{... | collective-permute-start | bytes 294920 | tf_op jit(solution)/shard_map/ppermute | solution.py:16
  10.7 0.2 collective-permute-start.22
  10.9 0.8 %compare_reduce_fusion = (pred[4,4]{1,0:T(4,128)(4,1)S(1)}, pred[4,4]{1,0:T(4,128)(4,1)S(1)}) fusion(s32[4,4]{1,0:T(4,128)S(1)} %collective-permute-done.19, s32[4]{0:T(128)S(1)} %iota_add_fusion, s32[4,4]{1,0:T(4,128)} %param.7), kind=kLoop, calls=%fused_computation.140 | loop fusion | flops 224 | bytes 176 | tf_op jit(solution)/shard_map/reduce_or | solution.py:167
  11.8 0.3 convolution_compare_fusion
  12.3 0.6 collective-permute-start.18
  12.9 0.3 convolution_compare_fusion.1
  13.2 4.8 %collective-permute-done.18 = bf16[128,768]{1,0:T(8,128)(2,1)S(1)} collective-permute-done((bf16[128,768]{1,0:T(8,128)(2,1)S(1)}, bf16[128,768]{1,0:T(8,128)(2,1)S(1)}, u32[]{:S(2)}, u32[]{:S(2)}) %collective-permute-start.18) | collective-permute-done | bytes 196640 | tf_op jit(solution)/shard_map/ppermute | solution.py:23
  18.0 0.9 %collective-permute-done.21 = bf16[64,768]{1,0:T(8,128)(2,1)S(1)} collective-permute-done((bf16[64,768]{1,0:T(8,128)(2,1)}, bf16[64,768]{1,0:T(8,128)(2,1)S(1)}, u32[]{:S(2)}, u32[]{:S(2)}) %collective-permute-start.21) | collective-permute-done | bytes 98336 | tf_op jit(solution)/shard_map/ppermute | solution.py:16
  18.9 0.5 collective-permute-start.24
  19.5 0.4 collective-permute-start.26
  20.5 0.3 collective-permute-done.25
  20.9 0.6 fusion.10
  21.8 0.6 fusion.11
  22.4 0.3 copy-done
  22.7 28.6 %collective-permute-start.29 = (f32[3,512]{1,0:T(4,128)S(1)}, f32[3,512]{1,0:T(4,128)S(1)}, u32[]{:S(2)}, u32[]{:S(2)}) collective-permute-start(f32[3,512]{1,0:T(4,128)S(1)} %get-tuple-element.104), channel_id=1, source_target_pairs={{0,4},{4,0},{8,12},{12,8},{16,20},{20,16},{24,28},{28,24},{1,5},{5... | collective-permute-start | bytes 18440 | tf_op jit(solution)/shard_map/ppermute | solution.py:16
  51.3 0.8 %collective-permute-done.29 = f32[3,512]{1,0:T(4,128)S(1)} collective-permute-done((f32[3,512]{1,0:T(4,128)S(1)}, f32[3,512]{1,0:T(4,128)S(1)}, u32[]{:S(2)}, u32[]{:S(2)}) %collective-permute-start.29) | collective-permute-done | bytes 6176 | tf_op jit(solution)/shard_map/ppermute | solution.py:16
  52.2 0.4 exponential_reduce_fusion.10
  52.6 0.4 fusion.16
  53.1 0.7 %copy-done.1 = bf16[512,768]{1,0:T(8,128)(2,1)S(1)} copy-done((bf16[512,768]{1,0:T(8,128)(2,1)S(1)}, bf16[512,768]{1,0:T(8,128)(2,1)}, u32[]{:S(2)}) %copy-start.1) | copy-done | bytes 786456
  53.8 0.4 convolution_add_fusion
  54.4 1.8 %collective-permute-start.32 = (bf16[72,768]{1,0:T(8,128)(2,1)S(1)}, bf16[72,768]{1,0:T(8,128)(2,1)S(1)}, u32[]{:S(2)}, u32[]{:S(2)}) collective-permute-start(bf16[72,768]{1,0:T(8,128)(2,1)S(1)} %get-tuple-element.92), channel_id=1, source_target_pairs={{0,24},{4,28},{8,16},{12,20},{16,8},{20,12},{24,0},{28,4},{1,25},{... | collective-permute-start | bytes 331784 | tf_op jit(solution)/shard_map/ppermute | solution.py:16
  56.2 0.8 %collective-permute-start.31 = (bf16[72,768]{1,0:T(8,128)(2,1)S(1)}, bf16[72,768]{1,0:T(8,128)(2,1)S(1)}, u32[]{:S(2)}, u32[]{:S(2)}) collective-permute-start(bf16[72,768]{1,0:T(8,128)(2,1)S(1)} %get-tuple-element.91), channel_id=1, source_target_pairs={{0,16},{4,20},{8,24},{12,28},{16,0},{20,4},{24,8},{28,12},{1,17},{... | collective-permute-start | bytes 331784 | tf_op jit(solution)/shard_map/ppermute | solution.py:16
  56.9 1.9 %collective-permute-start.30 = (bf16[72,768]{1,0:T(8,128)(2,1)S(1)}, bf16[72,768]{1,0:T(8,128)(2,1)S(1)}, u32[]{:S(2)}, u32[]{:S(2)}) collective-permute-start(bf16[72,768]{1,0:T(8,128)(2,1)S(1)} %get-tuple-element.90), channel_id=1, source_target_pairs={{0,8},{4,12},{8,0},{12,4},{16,24},{20,28},{24,16},{28,20},{1,9},{5... | collective-permute-start | bytes 331784 | tf_op jit(solution)/shard_map/ppermute | solution.py:16
  59.0 3.2 %collective-permute-done.32 = bf16[72,768]{1,0:T(8,128)(2,1)S(1)} collective-permute-done((bf16[72,768]{1,0:T(8,128)(2,1)S(1)}, bf16[72,768]{1,0:T(8,128)(2,1)S(1)}, u32[]{:S(2)}, u32[]{:S(2)}) %collective-permute-start.32) | collective-permute-done | bytes 110624 | tf_op jit(solution)/shard_map/ppermute | solution.py:16
  62.2 5.1 %collective-permute-done.31 = bf16[72,768]{1,0:T(8,128)(2,1)S(1)} collective-permute-done((bf16[72,768]{1,0:T(8,128)(2,1)S(1)}, bf16[72,768]{1,0:T(8,128)(2,1)S(1)}, u32[]{:S(2)}, u32[]{:S(2)}) %collective-permute-start.31) | collective-permute-done | bytes 110624 | tf_op jit(solution)/shard_map/ppermute | solution.py:16
  67.5 0.7 reshape.496
  68.3 0.6 pad_maximum_fusion.10
  68.9 0.7 %fusion.24 = bf16[64,768]{1,0:T(8,128)(2,1)} fusion(f32[1,4,64,768]{3,2,1,0:T(8,128)S(1)} %bitcast.67, s32[]{:T(128)S(6)} %select_n.199, bf16[72,768]{1,0:T(8,128)(2,1)S(1)} %collective-permute-done.32, bf16[72,768]{1,0:T(8,128)(2,1)S(1)} %collective-permute-done.31, bf16[72,768]{1,0:T(8,128)(2,1)S(1)} %collective-permute-done.30, f32[64]{0:T(128)S(1)} %fusion.58), kind=kLoop, calls=%fused_computation.116 | loop fusion | flops 393216 | bytes 590084 | tf_op jit(solution)/shard_map/convert_element_type | solution.py:241
  (83 shorter events, 1.9 us)
Async XLA Ops:
  0.6 11.5 %collective-permute-start.15 = (bf16[128,768]{1,0:T(8,128)(2,1)}, bf16[128,768]{1,0:T(8,128)(2,1)S(1)}, u32[]{:S(2)}, u32[]{:S(2)}) collective-permute-start(bf16[128,768]{1,0:T(8,128)(2,1)} %param.5), channel_id=1, source_target_pairs={{0,1},{1,0},{2,3},{3,2},{4,5},{5,4},{6,7},{7,6},{8,9},{9,8},{10,11... | collective-permute-start | bytes 589832 | tf_op jit(solution)/shard_map/ppermute | solution.py:16
  3.6 8.5 %collective-permute-start.16 = (bf16[128,768]{1,0:T(8,128)(2,1)}, bf16[128,768]{1,0:T(8,128)(2,1)S(1)}, u32[]{:S(2)}, u32[]{:S(2)}) collective-permute-start(bf16[128,768]{1,0:T(8,128)(2,1)} %param.5), channel_id=1, source_target_pairs={{0,2},{1,3},{2,0},{3,1},{4,6},{5,7},{6,4},{7,5},{8,10},{9,11},{10,... | collective-permute-start | bytes 589832 | tf_op jit(solution)/shard_map/ppermute | solution.py:16
  5.2 1.4 %collective-permute-start.19 = (s32[4,4]{1,0:T(4,128)}, s32[4,4]{1,0:T(4,128)S(1)}, u32[]{:S(2)}, u32[]{:S(2)}) collective-permute-start(s32[4,4]{1,0:T(4,128)} %param.7), channel_id=1, source_target_pairs={{0,4},{4,0},{8,12},{12,8},{16,20},{20,16},{24,28},{28,24},{1,5},{5... | collective-permute-start | bytes 200 | tf_op jit(solution)/shard_map/ppermute | solution.py:16
  6.5 11.5 %collective-permute-start.20 = (bf16[64,768]{1,0:T(8,128)(2,1)}, bf16[64,768]{1,0:T(8,128)(2,1)S(1)}, u32[]{:S(2)}, u32[]{:S(2)}) collective-permute-start(bf16[64,768]{1,0:T(8,128)(2,1)} %param.6), channel_id=1, source_target_pairs={{0,8},{4,12},{8,0},{12,4},{16,24},{20,28},{24,16},{28,20},{1,9},{5... | collective-permute-start | bytes 294920 | tf_op jit(solution)/shard_map/ppermute | solution.py:16
  8.1 10.8 %collective-permute-start.21 = (bf16[64,768]{1,0:T(8,128)(2,1)}, bf16[64,768]{1,0:T(8,128)(2,1)S(1)}, u32[]{:S(2)}, u32[]{:S(2)}) collective-permute-start(bf16[64,768]{1,0:T(8,128)(2,1)} %param.6), channel_id=1, source_target_pairs={{0,16},{4,20},{8,24},{12,28},{16,0},{20,4},{24,8},{28,12},{1,17},{... | collective-permute-start | bytes 294920 | tf_op jit(solution)/shard_map/ppermute | solution.py:16
  10.7 8.2 %collective-permute-start.22 = (bf16[64,768]{1,0:T(8,128)(2,1)}, bf16[64,768]{1,0:T(8,128)(2,1)S(1)}, u32[]{:S(2)}, u32[]{:S(2)}) collective-permute-start(bf16[64,768]{1,0:T(8,128)(2,1)} %param.6), channel_id=1, source_target_pairs={{0,24},{4,28},{8,16},{12,20},{16,8},{20,12},{24,0},{28,4},{1,25},{... | collective-permute-start | bytes 294920 | tf_op jit(solution)/shard_map/ppermute | solution.py:16
  12.2 5.8 %collective-permute-start.17 = (bf16[256,768]{1,0:T(8,128)(2,1)S(1)}, bf16[256,768]{1,0:T(8,128)(2,1)S(1)}, u32[]{:S(2)}, u32[]{:S(2)}) collective-permute-start(bf16[256,768]{1,0:T(8,128)(2,1)S(1)} %pad_maximum_fusion.8), channel_id=1, source_target_pairs={{0,4},{4,0},{8,12},{12,8},{16,20},{20,16},{24,28},{28,24},{1,5},{5... | collective-permute-start | bytes 1179656 | tf_op jit(solution)/shard_map/ppermute | solution.py:16
  12.3 5.7 %collective-permute-start.18 = (bf16[128,768]{1,0:T(8,128)(2,1)S(1)}, bf16[128,768]{1,0:T(8,128)(2,1)S(1)}, u32[]{:S(2)}, u32[]{:S(2)}) collective-permute-start(bf16[128,768]{1,0:T(8,128)(2,1)S(1)} %broadcast_select_fusion), channel_id=1, source_target_pairs={{0,2},{1,3},{2,0},{3,1},{4,5},{5,4},{6,7},{7,6},{8,10},{9,11},{10,... | collective-permute-start | bytes 589832 | tf_op jit(solution)/shard_map/ppermute | solution.py:23
  12.9 6.1 %copy-start.3 = (bf16[64,768]{1,0:T(8,128)(2,1)S(1)}, bf16[64,768]{1,0:T(8,128)(2,1)}, u32[]{:S(2)}) copy-start(bf16[64,768]{1,0:T(8,128)(2,1)} %param.6) | copy-start | bytes 294916
  12.9 7.1 %copy-start.2 = (bf16[128,768]{1,0:T(8,128)(2,1)S(1)}, bf16[128,768]{1,0:T(8,128)(2,1)}, u32[]{:S(2)}) copy-start(bf16[128,768]{1,0:T(8,128)(2,1)} %param.5) | copy-start | bytes 589828
  18.0 3.7 %collective-permute-start.28 = (bf16[128,768]{1,0:T(8,128)(2,1)S(1)}, bf16[128,768]{1,0:T(8,128)(2,1)S(1)}, u32[]{:S(2)}, u32[]{:S(2)}) collective-permute-start(bf16[128,768]{1,0:T(8,128)(2,1)S(1)} %collective-permute-done.18), channel_id=1, source_target_pairs={{0,4},{4,0},{8,12},{12,8},{16,20},{20,16},{24,28},{28,24},{1,5},{5... | collective-permute-start | bytes 589832 | tf_op jit(solution)/shard_map/ppermute | solution.py:16
  18.9 1.3 %collective-permute-start.23 = (bf16[64,768]{1,0:T(8,128)(2,1)S(1)}, bf16[64,768]{1,0:T(8,128)(2,1)S(1)}, u32[]{:S(2)}, u32[]{:S(2)}) collective-permute-start(bf16[64,768]{1,0:T(8,128)(2,1)S(1)} %copy-done.3), channel_id=1, source_target_pairs={{0,4},{4,0},{8,12},{12,8},{16,20},{20,16},{24,28},{28,24},{1,5},{5... | collective-permute-start | bytes 294920 | tf_op jit(solution)/shard_map/ppermute | solution.py:16
  18.9 1.5 %collective-permute-start.24 = (bf16[64,768]{1,0:T(8,128)(2,1)S(1)}, bf16[64,768]{1,0:T(8,128)(2,1)S(1)}, u32[]{:S(2)}, u32[]{:S(2)}) collective-permute-start(bf16[64,768]{1,0:T(8,128)(2,1)S(1)} %collective-permute-done.20), channel_id=1, source_target_pairs={{0,4},{4,0},{8,12},{12,8},{16,20},{20,16},{24,28},{28,24},{1,5},{5... | collective-permute-start | bytes 294920 | tf_op jit(solution)/shard_map/ppermute | solution.py:16
  19.5 1.3 %collective-permute-start.25 = (bf16[64,768]{1,0:T(8,128)(2,1)S(1)}, bf16[64,768]{1,0:T(8,128)(2,1)S(1)}, u32[]{:S(2)}, u32[]{:S(2)}) collective-permute-start(bf16[64,768]{1,0:T(8,128)(2,1)S(1)} %collective-permute-done.21), channel_id=1, source_target_pairs={{0,4},{4,0},{8,12},{12,8},{16,20},{20,16},{24,28},{28,24},{1,5},{5... | collective-permute-start | bytes 294920 | tf_op jit(solution)/shard_map/ppermute | solution.py:16
  19.5 1.4 %collective-permute-start.26 = (bf16[64,768]{1,0:T(8,128)(2,1)S(1)}, bf16[64,768]{1,0:T(8,128)(2,1)S(1)}, u32[]{:S(2)}, u32[]{:S(2)}) collective-permute-start(bf16[64,768]{1,0:T(8,128)(2,1)S(1)} %collective-permute-done.22), channel_id=1, source_target_pairs={{0,4},{4,0},{8,12},{12,8},{16,20},{20,16},{24,28},{28,24},{1,5},{5... | collective-permute-start | bytes 294920 | tf_op jit(solution)/shard_map/ppermute | solution.py:16
  20.2 1.5 %collective-permute-start.27 = (bf16[128,768]{1,0:T(8,128)(2,1)S(1)}, bf16[128,768]{1,0:T(8,128)(2,1)S(1)}, u32[]{:S(2)}, u32[]{:S(2)}) collective-permute-start(bf16[128,768]{1,0:T(8,128)(2,1)S(1)} %copy-done.2), channel_id=1, source_target_pairs={{0,4},{4,0},{8,12},{12,8},{16,20},{20,16},{24,28},{28,24},{1,5},{5... | collective-permute-start | bytes 589832 | tf_op jit(solution)/shard_map/ppermute | solution.py:16
  21.8 0.9 %copy-start = (bf16[512,768]{1,0:T(8,128)(2,1)}, bf16[512,768]{1,0:T(8,128)(2,1)S(1)}, u32[]{:S(2)}) copy-start(bf16[512,768]{1,0:T(8,128)(2,1)S(1)} %constant_dynamic-update-slice_fusion.52) | copy-start | bytes 2359300
  22.7 29.4 %collective-permute-start.29 = (f32[3,512]{1,0:T(4,128)S(1)}, f32[3,512]{1,0:T(4,128)S(1)}, u32[]{:S(2)}, u32[]{:S(2)}) collective-permute-start(f32[3,512]{1,0:T(4,128)S(1)} %get-tuple-element.104), channel_id=1, source_target_pairs={{0,4},{4,0},{8,12},{12,8},{16,20},{20,16},{24,28},{28,24},{1,5},{5... | collective-permute-start | bytes 18440 | tf_op jit(solution)/shard_map/ppermute | solution.py:16
  52.6 1.1 %copy-start.1 = (bf16[512,768]{1,0:T(8,128)(2,1)S(1)}, bf16[512,768]{1,0:T(8,128)(2,1)}, u32[]{:S(2)}) copy-start(bf16[512,768]{1,0:T(8,128)(2,1)} %copy-done) | copy-start | bytes 2359300
  54.4 7.9 %collective-permute-start.32 = (bf16[72,768]{1,0:T(8,128)(2,1)S(1)}, bf16[72,768]{1,0:T(8,128)(2,1)S(1)}, u32[]{:S(2)}, u32[]{:S(2)}) collective-permute-start(bf16[72,768]{1,0:T(8,128)(2,1)S(1)} %get-tuple-element.92), channel_id=1, source_target_pairs={{0,24},{4,28},{8,16},{12,20},{16,8},{20,12},{24,0},{28,4},{1,25},{... | collective-permute-start | bytes 331784 | tf_op jit(solution)/shard_map/ppermute | solution.py:16
  56.2 11.2 %collective-permute-start.31 = (bf16[72,768]{1,0:T(8,128)(2,1)S(1)}, bf16[72,768]{1,0:T(8,128)(2,1)S(1)}, u32[]{:S(2)}, u32[]{:S(2)}) collective-permute-start(bf16[72,768]{1,0:T(8,128)(2,1)S(1)} %get-tuple-element.91), channel_id=1, source_target_pairs={{0,16},{4,20},{8,24},{12,28},{16,0},{20,4},{24,8},{28,12},{1,17},{... | collective-permute-start | bytes 331784 | tf_op jit(solution)/shard_map/ppermute | solution.py:16
  56.9 10.4 %collective-permute-start.30 = (bf16[72,768]{1,0:T(8,128)(2,1)S(1)}, bf16[72,768]{1,0:T(8,128)(2,1)S(1)}, u32[]{:S(2)}, u32[]{:S(2)}) collective-permute-start(bf16[72,768]{1,0:T(8,128)(2,1)S(1)} %get-tuple-element.90), channel_id=1, source_target_pairs={{0,8},{4,12},{8,0},{12,4},{16,24},{20,28},{24,16},{28,20},{1,9},{5... | collective-permute-start | bytes 331784 | tf_op jit(solution)/shard_map/ppermute | solution.py:16

commit v3 on v2

--- a/solution.py
+++ b/solution.py
@@ -235,12 +235,14 @@
             masses.append(from_thirds(got[block.shape[0] :], group_cols))
         held, mass = add(parts), add(masses)
     own_mass = lax.dynamic_slice_in_dim(mass, me_row // 2 * per, per, 0)
-    col_pots = (col_pot + math.log(target) - jnp.log(mass)).reshape(2, chips, per)
-    col_pots = jnp.where(core == 1, col_pots[::-1], col_pots)
+    col_pots = col_pot + math.log(target) - jnp.log(mass)
+    pieces = jnp.split(col_pots, 2 * chips)
+    pieces = [jnp.where(core == 1, pieces[n - chips], piece) for n, piece in enumerate(pieces)]
+    col_pots = jnp.concatenate([pieces[n] for chip in range(chips) for n in (chip, chips + chip)])
     return (
         (held.reshape(per, width) * (target * mass_ratio / own_mass)[:, None]).astype(jnp.bfloat16),
         row_out,
-        col_pots.swapaxes(0, 1).reshape(-1),
+        col_pots,
     )
 
 

time: 69.8 us -> 72.9 us (1.044)
  starting transfers between devices: 43.8 us -> 45.1 us
  local copies, waits for them, and re-layouts: 2.47 us -> 3.28 us
  waiting for transfers between devices: 16.8 us -> 17.6 us
    ppermute x17, starting transfers between devices: 43.2 us -> 44.5 us  [swap(): lax.ppermute(x, axis, [(i, i ^ k) for i in range(lax.axis_size(axis))])]
    slice x0 -> x2, local copies, waits for them, and re-layouts: none -> 1.17 us  [the longest x1 0.59 us: per_device(): known[:-1].reshape(-1)]
    ppermute x17, waiting for transfers between devices: 12 us -> 12.8 us  [swap(): lax.ppermute(x, axis, [(i, i ^ k) for i in range(lax.axis_size(axis))])]
  transfers between devices with their start and end apart: 18 -> 18, of which waited for: 10 -> 10; matrix products, arithmetic and copies ran while one was open for 4% -> 3% of each run, Pallas kernels for 0% -> 0%
where the time goes in v3:
time: 72.9 us; the launch traced here: 72.6 us
  starting transfers between devices  45.1 us (62%)
  waiting for transfers between devices  17.6 us (24%)
  local copies, waits for them, and re-layouts  3.28 us (4%)
  other arithmetic  2.95 us (4%)
  matrix products  2.57 us (4%)
  between operations  1.06 us (1%)
    ppermute x17, starting transfers between devices, swap(): lax.ppermute(x, axis, [(i, i ^ k) for i in range(lax.axis_size(axis))])  44.5 us
    ppermute x17, waiting for transfers between devices, swap(): lax.ppermute(x, axis, [(i, i ^ k) for i in range(lax.axis_size(axis))])  12.8 us
    ppermute x1, waiting for transfers between devices, swap_by_core(): return lax.ppermute(x, ('row', 'col'), pairs)  4.83 us
  transfers between devices with their start and end apart: 18, of which 10 were waited for; matrix products, arithmetic and copies ran while one was open for 3% of the time, Pallas kernels for 0%

profile of v3, /device:TPU:0, one launch (start us, length us, event | category | flops | bytes accessed | tf_op | source)
XLA Modules:
  0.0 72.6 jit_solution(8041611221109170987)
XLA Ops:
  0.6 3.0 %collective-permute-start.15 = (bf16[128,768]{1,0:T(8,128)(2,1)}, bf16[128,768]{1,0:T(8,128)(2,1)S(1)}, u32[]{:S(2)}, u32[]{:S(2)}) collective-permute-start(bf16[128,768]{1,0:T(8,128)(2,1)} %param.5), channel_id=1, source_target_pairs={{0,1},{1,0},{2,3},{3,2},{4,5},{5,4},{6,7},{7,6},{8,9},{9,8},{10,11... | collective-permute-start | bytes 589832 | tf_op jit(solution)/shard_map/ppermute | solution.py:16
  3.6 1.5 %collective-permute-start.16 = (bf16[128,768]{1,0:T(8,128)(2,1)}, bf16[128,768]{1,0:T(8,128)(2,1)S(1)}, u32[]{:S(2)}, u32[]{:S(2)}) collective-permute-start(bf16[128,768]{1,0:T(8,128)(2,1)} %param.5), channel_id=1, source_target_pairs={{0,2},{1,3},{2,0},{3,1},{4,6},{5,7},{6,4},{7,5},{8,10},{9,11},{10,... | collective-permute-start | bytes 589832 | tf_op jit(solution)/shard_map/ppermute | solution.py:16
  5.2 1.3 %collective-permute-done.19 = s32[4,4]{1,0:T(4,128)S(1)} collective-permute-done((s32[4,4]{1,0:T(4,128)}, s32[4,4]{1,0:T(4,128)S(1)}, u32[]{:S(2)}, u32[]{:S(2)}) %collective-permute-start.19) | collective-permute-done | bytes 96 | tf_op jit(solution)/shard_map/ppermute | solution.py:16
  6.5 1.6 %collective-permute-start.20 = (bf16[64,768]{1,0:T(8,128)(2,1)}, bf16[64,768]{1,0:T(8,128)(2,1)S(1)}, u32[]{:S(2)}, u32[]{:S(2)}) collective-permute-start(bf16[64,768]{1,0:T(8,128)(2,1)} %param.6), channel_id=1, source_target_pairs={{0,8},{4,12},{8,0},{12,4},{16,24},{20,28},{24,16},{28,20},{1,9},{5... | collective-permute-start | bytes 294920 | tf_op jit(solution)/shard_map/ppermute | solution.py:16
  8.1 2.6 %collective-permute-start.21 = (bf16[64,768]{1,0:T(8,128)(2,1)}, bf16[64,768]{1,0:T(8,128)(2,1)S(1)}, u32[]{:S(2)}, u32[]{:S(2)}) collective-permute-start(bf16[64,768]{1,0:T(8,128)(2,1)} %param.6), channel_id=1, source_target_pairs={{0,16},{4,20},{8,24},{12,28},{16,0},{20,4},{24,8},{28,12},{1,17},{... | collective-permute-start | bytes 294920 | tf_op jit(solution)/shard_map/ppermute | solution.py:16
  10.9 0.8 %compare_reduce_fusion = (pred[4,4]{1,0:T(4,128)(4,1)S(1)}, pred[4,4]{1,0:T(4,128)(4,1)S(1)}) fusion(s32[4,4]{1,0:T(4,128)S(1)} %collective-permute-done.19, s32[4]{0:T(128)S(1)} %iota_add_fusion, s32[4,4]{1,0:T(4,128)} %param.7), kind=kLoop, calls=%fused_computation.140 | loop fusion | flops 224 | bytes 176 | tf_op jit(solution)/shard_map/reduce_or | solution.py:167
  12.3 0.6 collective-permute-start.18
  12.9 0.3 convolution_compare_fusion.1
  13.2 4.8 %collective-permute-done.18 = bf16[128,768]{1,0:T(8,128)(2,1)S(1)} collective-permute-done((bf16[128,768]{1,0:T(8,128)(2,1)S(1)}, bf16[128,768]{1,0:T(8,128)(2,1)S(1)}, u32[]{:S(2)}, u32[]{:S(2)}) %collective-permute-start.18) | collective-permute-done | bytes 196640 | tf_op jit(solution)/shard_map/ppermute | solution.py:23
  18.0 0.9 %collective-permute-done.21 = bf16[64,768]{1,0:T(8,128)(2,1)S(1)} collective-permute-done((bf16[64,768]{1,0:T(8,128)(2,1)}, bf16[64,768]{1,0:T(8,128)(2,1)S(1)}, u32[]{:S(2)}, u32[]{:S(2)}) %collective-permute-start.21) | collective-permute-done | bytes 98336 | tf_op jit(solution)/shard_map/ppermute | solution.py:16
  18.9 0.5 collective-permute-start.24
  19.5 0.4 collective-permute-start.26
  20.9 0.6 fusion.10
  21.8 0.6 fusion.11
  22.4 0.3 copy-done
  22.7 1.2 %conditional.1 = (f32[3,512]{1,0:T(4,128)S(1)}, f32[2,512]{1,0:T(2,128)}, f32[1,512]{1,0:T(1,128)}, f32[1024]{0:T(1024)S(1)}, f32[512]{0:T(512)S(1)}) conditional(s32[]{:T(128)} %convert_element_type.105, () %tuple.34, (f32[512,512]{1,0:T(8,128)S(1)}, f32[512,512]{1,0:T(8,128)S(1)}) %tuple.36), branch_computations={%region_2.3_spmd, %region_3.18_spmd} | conditional | flops 8969728 | bytes 15288968 | solution.py:205
  22.7 0.6 slice.401
  23.3 0.6 slice.402
  23.9 29.9 %collective-permute-start.29 = (f32[3,512]{1,0:T(4,128)S(1)}, f32[3,512]{1,0:T(4,128)S(1)}, u32[]{:S(2)}, u32[]{:S(2)}) collective-permute-start(f32[3,512]{1,0:T(4,128)S(1)} %get-tuple-element.40), channel_id=1, source_target_pairs={{0,4},{4,0},{8,12},{12,8},{16,20},{20,16},{24,28},{28,24},{1,5},{5... | collective-permute-start | bytes 18440 | tf_op jit(solution)/shard_map/ppermute | solution.py:16
  53.8 0.8 %collective-permute-done.29 = f32[3,512]{1,0:T(4,128)S(1)} collective-permute-done((f32[3,512]{1,0:T(4,128)S(1)}, f32[3,512]{1,0:T(4,128)S(1)}, u32[]{:S(2)}, u32[]{:S(2)}) %collective-permute-start.29) | collective-permute-done | bytes 6176 | tf_op jit(solution)/shard_map/ppermute | solution.py:16
  54.7 0.4 exponential_reduce_fusion.10
  55.2 0.4 fusion.16
  55.6 0.7 copy-done.1
  56.3 0.4 convolution_add_fusion
  56.9 1.8 %collective-permute-start.32 = (bf16[72,768]{1,0:T(8,128)(2,1)S(1)}, bf16[72,768]{1,0:T(8,128)(2,1)S(1)}, u32[]{:S(2)}, u32[]{:S(2)}) collective-permute-start(bf16[72,768]{1,0:T(8,128)(2,1)S(1)} %get-tuple-element.99), channel_id=1, source_target_pairs={{0,24},{4,28},{8,16},{12,20},{16,8},{20,12},{24,0},{28,4},{1,25},{... | collective-permute-start | bytes 331784 | tf_op jit(solution)/shard_map/ppermute | solution.py:16
  58.7 0.8 %collective-permute-start.31 = (bf16[72,768]{1,0:T(8,128)(2,1)S(1)}, bf16[72,768]{1,0:T(8,128)(2,1)S(1)}, u32[]{:S(2)}, u32[]{:S(2)}) collective-permute-start(bf16[72,768]{1,0:T(8,128)(2,1)S(1)} %get-tuple-element.98), channel_id=1, source_target_pairs={{0,16},{4,20},{8,24},{12,28},{16,0},{20,4},{24,8},{28,12},{1,17},{... | collective-permute-start | bytes 331784 | tf_op jit(solution)/shard_map/ppermute | solution.py:16
  59.4 1.9 %collective-permute-start.30 = (bf16[72,768]{1,0:T(8,128)(2,1)S(1)}, bf16[72,768]{1,0:T(8,128)(2,1)S(1)}, u32[]{:S(2)}, u32[]{:S(2)}) collective-permute-start(bf16[72,768]{1,0:T(8,128)(2,1)S(1)} %get-tuple-element.97), channel_id=1, source_target_pairs={{0,8},{4,12},{8,0},{12,4},{16,24},{20,28},{24,16},{28,20},{1,9},{5... | collective-permute-start | bytes 331784 | tf_op jit(solution)/shard_map/ppermute | solution.py:16
  61.3 3.5 %collective-permute-done.32 = bf16[72,768]{1,0:T(8,128)(2,1)S(1)} collective-permute-done((bf16[72,768]{1,0:T(8,128)(2,1)S(1)}, bf16[72,768]{1,0:T(8,128)(2,1)S(1)}, u32[]{:S(2)}, u32[]{:S(2)}) %collective-permute-start.32) | collective-permute-done | bytes 110624 | tf_op jit(solution)/shard_map/ppermute | solution.py:16
  64.8 5.6 %collective-permute-done.31 = bf16[72,768]{1,0:T(8,128)(2,1)S(1)} collective-permute-done((bf16[72,768]{1,0:T(8,128)(2,1)S(1)}, bf16[72,768]{1,0:T(8,128)(2,1)S(1)}, u32[]{:S(2)}, u32[]{:S(2)}) %collective-permute-start.31) | collective-permute-done | bytes 110624 | tf_op jit(solution)/shard_map/ppermute | solution.py:16
  70.6 0.6 pad_maximum_fusion.10
  71.2 0.7 concatenate.97
  71.9 0.7 fusion.24
  (80 shorter events, 2.4 us)
Async XLA Ops:
  0.6 11.5 %collective-permute-start.15 = (bf16[128,768]{1,0:T(8,128)(2,1)}, bf16[128,768]{1,0:T(8,128)(2,1)S(1)}, u32[]{:S(2)}, u32[]{:S(2)}) collective-permute-start(bf16[128,768]{1,0:T(8,128)(2,1)} %param.5), channel_id=1, source_target_pairs={{0,1},{1,0},{2,3},{3,2},{4,5},{5,4},{6,7},{7,6},{8,9},{9,8},{10,11... | collective-permute-start | bytes 589832 | tf_op jit(solution)/shard_map/ppermute | solution.py:16
  3.6 8.5 %collective-permute-start.16 = (bf16[128,768]{1,0:T(8,128)(2,1)}, bf16[128,768]{1,0:T(8,128)(2,1)S(1)}, u32[]{:S(2)}, u32[]{:S(2)}) collective-permute-start(bf16[128,768]{1,0:T(8,128)(2,1)} %param.5), channel_id=1, source_target_pairs={{0,2},{1,3},{2,0},{3,1},{4,6},{5,7},{6,4},{7,5},{8,10},{9,11},{10,... | collective-permute-start | bytes 589832 | tf_op jit(solution)/shard_map/ppermute | solution.py:16
  5.2 1.4 %collective-permute-start.19 = (s32[4,4]{1,0:T(4,128)}, s32[4,4]{1,0:T(4,128)S(1)}, u32[]{:S(2)}, u32[]{:S(2)}) collective-permute-start(s32[4,4]{1,0:T(4,128)} %param.7), channel_id=1, source_target_pairs={{0,4},{4,0},{8,12},{12,8},{16,20},{20,16},{24,28},{28,24},{1,5},{5... | collective-permute-start | bytes 200 | tf_op jit(solution)/shard_map/ppermute | solution.py:16
  6.5 11.5 %collective-permute-start.20 = (bf16[64,768]{1,0:T(8,128)(2,1)}, bf16[64,768]{1,0:T(8,128)(2,1)S(1)}, u32[]{:S(2)}, u32[]{:S(2)}) collective-permute-start(bf16[64,768]{1,0:T(8,128)(2,1)} %param.6), channel_id=1, source_target_pairs={{0,8},{4,12},{8,0},{12,4},{16,24},{20,28},{24,16},{28,20},{1,9},{5... | collective-permute-start | bytes 294920 | tf_op jit(solution)/shard_map/ppermute | solution.py:16
  8.1 10.8 %collective-permute-start.21 = (bf16[64,768]{1,0:T(8,128)(2,1)}, bf16[64,768]{1,0:T(8,128)(2,1)S(1)}, u32[]{:S(2)}, u32[]{:S(2)}) collective-permute-start(bf16[64,768]{1,0:T(8,128)(2,1)} %param.6), channel_id=1, source_target_pairs={{0,16},{4,20},{8,24},{12,28},{16,0},{20,4},{24,8},{28,12},{1,17},{... | collective-permute-start | bytes 294920 | tf_op jit(solution)/shard_map/ppermute | solution.py:16
  10.7 8.2 %collective-permute-start.22 = (bf16[64,768]{1,0:T(8,128)(2,1)}, bf16[64,768]{1,0:T(8,128)(2,1)S(1)}, u32[]{:S(2)}, u32[]{:S(2)}) collective-permute-start(bf16[64,768]{1,0:T(8,128)(2,1)} %param.6), channel_id=1, source_target_pairs={{0,24},{4,28},{8,16},{12,20},{16,8},{20,12},{24,0},{28,4},{1,25},{... | collective-permute-start | bytes 294920 | tf_op jit(solution)/shard_map/ppermute | solution.py:16
  12.2 5.8 %collective-permute-start.17 = (bf16[256,768]{1,0:T(8,128)(2,1)S(1)}, bf16[256,768]{1,0:T(8,128)(2,1)S(1)}, u32[]{:S(2)}, u32[]{:S(2)}) collective-permute-start(bf16[256,768]{1,0:T(8,128)(2,1)S(1)} %pad_maximum_fusion.8), channel_id=1, source_target_pairs={{0,4},{4,0},{8,12},{12,8},{16,20},{20,16},{24,28},{28,24},{1,5},{5... | collective-permute-start | bytes 1179656 | tf_op jit(solution)/shard_map/ppermute | solution.py:16
  12.3 5.7 %collective-permute-start.18 = (bf16[128,768]{1,0:T(8,128)(2,1)S(1)}, bf16[128,768]{1,0:T(8,128)(2,1)S(1)}, u32[]{:S(2)}, u32[]{:S(2)}) collective-permute-start(bf16[128,768]{1,0:T(8,128)(2,1)S(1)} %broadcast_select_fusion), channel_id=1, source_target_pairs={{0,2},{1,3},{2,0},{3,1},{4,5},{5,4},{6,7},{7,6},{8,10},{9,11},{10,... | collective-permute-start | bytes 589832 | tf_op jit(solution)/shard_map/ppermute | solution.py:23
  12.9 6.1 %copy-start.3 = (bf16[64,768]{1,0:T(8,128)(2,1)S(1)}, bf16[64,768]{1,0:T(8,128)(2,1)}, u32[]{:S(2)}) copy-start(bf16[64,768]{1,0:T(8,128)(2,1)} %param.6) | copy-start | bytes 294916
  12.9 7.1 %copy-start.2 = (bf16[128,768]{1,0:T(8,128)(2,1)S(1)}, bf16[128,768]{1,0:T(8,128)(2,1)}, u32[]{:S(2)}) copy-start(bf16[128,768]{1,0:T(8,128)(2,1)} %param.5) | copy-start | bytes 589828
  18.0 3.7 %collective-permute-start.28 = (bf16[128,768]{1,0:T(8,128)(2,1)S(1)}, bf16[128,768]{1,0:T(8,128)(2,1)S(1)}, u32[]{:S(2)}, u32[]{:S(2)}) collective-permute-start(bf16[128,768]{1,0:T(8,128)(2,1)S(1)} %collective-permute-done.18), channel_id=1, source_target_pairs={{0,4},{4,0},{8,12},{12,8},{16,20},{20,16},{24,28},{28,24},{1,5},{5... | collective-permute-start | bytes 589832 | tf_op jit(solution)/shard_map/ppermute | solution.py:16
  18.9 1.3 %collective-permute-start.23 = (bf16[64,768]{1,0:T(8,128)(2,1)S(1)}, bf16[64,768]{1,0:T(8,128)(2,1)S(1)}, u32[]{:S(2)}, u32[]{:S(2)}) collective-permute-start(bf16[64,768]{1,0:T(8,128)(2,1)S(1)} %copy-done.3), channel_id=1, source_target_pairs={{0,4},{4,0},{8,12},{12,8},{16,20},{20,16},{24,28},{28,24},{1,5},{5... | collective-permute-start | bytes 294920 | tf_op jit(solution)/shard_map/ppermute | solution.py:16
  18.9 1.5 %collective-permute-start.24 = (bf16[64,768]{1,0:T(8,128)(2,1)S(1)}, bf16[64,768]{1,0:T(8,128)(2,1)S(1)}, u32[]{:S(2)}, u32[]{:S(2)}) collective-permute-start(bf16[64,768]{1,0:T(8,128)(2,1)S(1)} %collective-permute-done.20), channel_id=1, source_target_pairs={{0,4},{4,0},{8,12},{12,8},{16,20},{20,16},{24,28},{28,24},{1,5},{5... | collective-permute-start | bytes 294920 | tf_op jit(solution)/shard_map/ppermute | solution.py:16
  19.5 1.3 %collective-permute-start.25 = (bf16[64,768]{1,0:T(8,128)(2,1)S(1)}, bf16[64,768]{1,0:T(8,128)(2,1)S(1)}, u32[]{:S(2)}, u32[]{:S(2)}) collective-permute-start(bf16[64,768]{1,0:T(8,128)(2,1)S(1)} %collective-permute-done.21), channel_id=1, source_target_pairs={{0,4},{4,0},{8,12},{12,8},{16,20},{20,16},{24,28},{28,24},{1,5},{5... | collective-permute-start | bytes 294920 | tf_op jit(solution)/shard_map/ppermute | solution.py:16
  19.5 1.4 %collective-permute-start.26 = (bf16[64,768]{1,0:T(8,128)(2,1)S(1)}, bf16[64,768]{1,0:T(8,128)(2,1)S(1)}, u32[]{:S(2)}, u32[]{:S(2)}) collective-permute-start(bf16[64,768]{1,0:T(8,128)(2,1)S(1)} %collective-permute-done.22), channel_id=1, source_target_pairs={{0,4},{4,0},{8,12},{12,8},{16,20},{20,16},{24,28},{28,24},{1,5},{5... | collective-permute-start | bytes 294920 | tf_op jit(solution)/shard_map/ppermute | solution.py:16
  20.2 1.5 %collective-permute-start.27 = (bf16[128,768]{1,0:T(8,128)(2,1)S(1)}, bf16[128,768]{1,0:T(8,128)(2,1)S(1)}, u32[]{:S(2)}, u32[]{:S(2)}) collective-permute-start(bf16[128,768]{1,0:T(8,128)(2,1)S(1)} %copy-done.2), channel_id=1, source_target_pairs={{0,4},{4,0},{8,12},{12,8},{16,20},{20,16},{24,28},{28,24},{1,5},{5... | collective-permute-start | bytes 589832 | tf_op jit(solution)/shard_map/ppermute | solution.py:16
  21.8 0.9 %copy-start = (bf16[512,768]{1,0:T(8,128)(2,1)}, bf16[512,768]{1,0:T(8,128)(2,1)S(1)}, u32[]{:S(2)}) copy-start(bf16[512,768]{1,0:T(8,128)(2,1)S(1)} %constant_dynamic-update-slice_fusion.52) | copy-start | bytes 2359300
  23.9 30.8 %collective-permute-start.29 = (f32[3,512]{1,0:T(4,128)S(1)}, f32[3,512]{1,0:T(4,128)S(1)}, u32[]{:S(2)}, u32[]{:S(2)}) collective-permute-start(f32[3,512]{1,0:T(4,128)S(1)} %get-tuple-element.40), channel_id=1, source_target_pairs={{0,4},{4,0},{8,12},{12,8},{16,20},{20,16},{24,28},{28,24},{1,5},{5... | collective-permute-start | bytes 18440 | tf_op jit(solution)/shard_map/ppermute | solution.py:16
  55.2 1.1 %copy-start.1 = (bf16[512,768]{1,0:T(8,128)(2,1)S(1)}, bf16[512,768]{1,0:T(8,128)(2,1)}, u32[]{:S(2)}) copy-start(bf16[512,768]{1,0:T(8,128)(2,1)} %copy-done) | copy-start | bytes 2359300
  56.9 7.9 %collective-permute-start.32 = (bf16[72,768]{1,0:T(8,128)(2,1)S(1)}, bf16[72,768]{1,0:T(8,128)(2,1)S(1)}, u32[]{:S(2)}, u32[]{:S(2)}) collective-permute-start(bf16[72,768]{1,0:T(8,128)(2,1)S(1)} %get-tuple-element.99), channel_id=1, source_target_pairs={{0,24},{4,28},{8,16},{12,20},{16,8},{20,12},{24,0},{28,4},{1,25},{... | collective-permute-start | bytes 331784 | tf_op jit(solution)/shard_map/ppermute | solution.py:16
  58.7 11.7 %collective-permute-start.31 = (bf16[72,768]{1,0:T(8,128)(2,1)S(1)}, bf16[72,768]{1,0:T(8,128)(2,1)S(1)}, u32[]{:S(2)}, u32[]{:S(2)}) collective-permute-start(bf16[72,768]{1,0:T(8,128)(2,1)S(1)} %get-tuple-element.98), channel_id=1, source_target_pairs={{0,16},{4,20},{8,24},{12,28},{16,0},{20,4},{24,8},{28,12},{1,17},{... | collective-permute-start | bytes 331784 | tf_op jit(solution)/shard_map/ppermute | solution.py:16
  59.4 11.0 %collective-permute-start.30 = (bf16[72,768]{1,0:T(8,128)(2,1)S(1)}, bf16[72,768]{1,0:T(8,128)(2,1)S(1)}, u32[]{:S(2)}, u32[]{:S(2)}) collective-permute-start(bf16[72,768]{1,0:T(8,128)(2,1)S(1)} %get-tuple-element.97), channel_id=1, source_target_pairs={{0,8},{4,12},{8,0},{12,4},{16,24},{20,28},{24,16},{28,20},{1,9},{5... | collective-permute-start | bytes 331784 | tf_op jit(solution)/shard_map/ppermute | solution.py:16
